TPU v7x, 512 devices: a whole 4x4x16 slice. The times are simulated.
512 devices in a mesh: turn: 128 (over y, x, z_lo), hand: 4 (over z_hi, core).
Axes of the slice: x: 4, y: 4, z: 16 (z_hi: 2, z_lo: 8; z = z_hi * 8 + z_lo), core: 2. Of those that a mesh axis runs over, the one named last changes fastest.
Arguments:
- reach: bfloat16 [512, 81, 1024], P('turn', None, 'hand'), may hold values from 0.019897461 to 1
- ranks: int32 [512, 1024], P('turn', 'hand'), may hold values from 0 to 7461
- live: int32 [512, 1024], P('turn', 'hand'), may hold values 0 or 1
- turn_of: int32 [512], P('turn'), may hold values from 0 to 48, never falling along the last dimension, each value on 1 to 48 neighbouring positions
- hand_cards: int32 [2, 1024], replicated, may hold values from 0 to 51, as said below
- pot: float32 [81], replicated, may hold values from 1 to 8
- turn_act: int32 [81], replicated, may hold values from 0 to 8
- flop_act: int32 [81], replicated, may hold values from 0 to 8
- turn_regret: float32 [49, 9, 1024], P(None, None, 'hand'), may hold values from 0.1 to 10
- flop_regret: float32 [9, 1024], P(None, 'hand'), may hold values from 0.05 to 5
Outputs:
- new_turn_regret: float32 [49, 9, 1024], P(None, None, 'hand')
- new_flop_regret: float32 [9, 1024], P(None, 'hand')
- turn_values: float32 [49, 1024], P(None, 'hand')
Inputs may be any that keep to these rules, and one draw needn't show every extreme that they name: `hand_cards`: each column holds two different cards of a 52-card deck, and no two hands are alike. `turn_of`: the boards of one turn card stand in a row, in rising order of turn card, at most 48 boards a turn card.
All inputs are finite; a program needn't handle non-finite values. No bound on the sum of `live` on one device may be relied on, other than what follows from the above.
Results may differ from a plain program's by a relative error of at most 0.0003.
Values may be sent and summed in bfloat16 or wider, within the bound.
No kernel may reach another device: no remote copies, remote signals or barrier semaphores. Data moves between devices by JAX's collectives and lax.ppermute only.
A program may use at most 64 MiB of HBM per device.

v0:
```python
import jax
import jax.numpy as jnp
from jax import lax
from jax.sharding import PartitionSpec as P


def card_apart(left, right):
    return (
        (left[0][:, None] != right[0][None, :])
        & (left[0][:, None] != right[1][None, :])
        & (left[1][:, None] != right[0][None, :])
        & (left[1][:, None] != right[1][None, :])
    ).astype(jnp.int32)


def shards(
    reach, ranks, live, turn_of, hand_cards, pot, turn_act, flop_act, turn_regret, flop_regret
):
    boards_here = reach.shape[0]
    width = reach.shape[2]
    total_hands = hand_cards.shape[1]
    turns = turn_regret.shape[0]
    actions = turn_regret.shape[1]
    own_codes = jnp.stack([ranks, live], axis=1)
    scale = pot[:, None] / total_hands
    turn_map = (turn_act[None, :] == jnp.arange(actions, dtype=jnp.int32)[:, None]).astype(
        jnp.float32
    )
    flop_map = (
        flop_act[None, :] == jnp.arange(flop_regret.shape[0], dtype=jnp.int32)[:, None]
    ).astype(jnp.float32)
    boards_all = boards_here * lax.axis_size("turn")
    own_cards = lax.dynamic_slice_in_dim(hand_cards, lax.axis_index("hand") * width, width, 1)
    reach_piece = lax.all_gather(reach, "hand", axis=2, tiled=True)
    code_piece = lax.all_gather(own_codes, "hand", axis=2, tiled=True)
    apart = card_apart(own_cards, hand_cards)

    def one_board(items):
        rows, mine, theirs = items
        tile = (
            jnp.sign(mine[0][:, None] - theirs[0][None, :])
            * mine[1][:, None]
            * theirs[1][None, :]
            * apart
        ).astype(jnp.bfloat16)
        return lax.dot_general(
            rows, tile, (((1,), (1,)), ((), ())), preferred_element_type=jnp.float32
        )

    summed = lax.map(one_board, (reach_piece, own_codes, code_piece))
    values = summed * scale[None, :, :]
    board_map = (turn_of[None, :] == jnp.arange(turns, dtype=jnp.int32)[:, None]).astype(
        jnp.float32
    )
    partial_values = jnp.einsum("tb,bsi->tsi", board_map, values, precision=lax.Precision.HIGHEST)
    seq_values = lax.psum(partial_values, "turn")
    q_sum = jnp.einsum("as,tsi->tai", turn_map, seq_values, precision=lax.Precision.HIGHEST)
    flop_sum = jnp.einsum(
        "fs,si->fi", flop_map, jnp.sum(seq_values, axis=0), precision=lax.Precision.HIGHEST
    )
    q_turn = q_sum * (turns / boards_all)
    flop_q = flop_sum / boards_all
    turn_values = jnp.sum(turn_regret * q_turn, axis=1) / jnp.sum(turn_regret, axis=1)
    new_turn_regret = jnp.maximum(turn_regret + q_turn - turn_values[:, None, :], 0.0)
    flop_value = jnp.sum(flop_regret * flop_q, axis=0) / jnp.sum(flop_regret, axis=0)
    new_flop_regret = jnp.maximum(flop_regret + flop_q - flop_value[None, :], 0.0)
    return (new_turn_regret, new_flop_regret, turn_values)


def solution(mesh):
    return jax.shard_map(
        shards,
        mesh=mesh,
        in_specs=(
            P("turn", None, "hand"),
            P("turn", "hand"),
            P("turn", "hand"),
            P("turn"),
            P(),
            P(),
            P(),
            P(),
            P(None, None, "hand"),
            P(None, "hand"),
        ),
        out_specs=(P(None, None, "hand"), P(None, "hand"), P(None, "hand")),
        check_vma=False,
    )
```

profile of v0, /device:TPU:0, one launch (start us, length us, event | category | flops | bytes accessed | tf_op | source)
XLA Modules:
  0.0 2073.3 jit_solution(2631411981681031091)
XLA Ops:
  7.2 0.0 all-reduce.2.cloned.1.call-start
  7.2 0.7 stack.10
  7.9 0.7 stack.9
  8.6 13.9 all_gather.7
  22.5 0.8 fusion.38
  23.3 0.9 copy.13
  24.2 17.4 all_gather.6
  41.6 0.8 fusion.37
  42.4 0.0 copy-start.6
  42.4 0.0 copy-start.3
  42.4 3.2 while.11
  42.5 0.8 fusion.43
  43.3 0.8 fusion.43
  44.1 0.8 fusion.43
  44.9 0.8 fusion.43
  45.7 0.0 copy-done.6
  45.7 0.1 broadcast_multiply_fusion
  45.8 0.0 copy-done.3
  45.8 0.0 copy-start
  45.8 0.0 copy-start.4
  45.8 4.2 fusion.27
  50.1 0.0 all-reduce.2.cloned.1.call-update
  50.1 0.0 copy-done
  50.2 2006.1 %all-reduce.2.cloned.1.call-done = f32[49,81,256]{2,0,1:T(8,128)} async-done(((f32[49,81,256]{2,0,1:T(8,128)}), f32[49,81,256]{2,0,1:T(8,128)}) %all-reduce.2.cloned.1.call-update) | async-done | bytes 4064272 | tf_op jit(solution)/shard_map/psum | solution.py:56
  2056.2 0.0 copy-done.4
  2056.2 5.2 fusion.26
  2061.4 0.0 copy-start.2
  2061.4 0.0 copy-start.5
  2061.4 0.0 copy-start.1
  2061.4 0.3 fusion.25
  2061.7 1.1 copy.18
  2062.8 2.9 reduce_sum.47
  2065.6 0.0 copy-done.2
  2065.6 0.0 copy-done.5
  2065.6 0.2 fusion.36
  2065.8 0.6 subtract_maximum_fusion
  2066.4 0.0 copy-done.1
  (14 shorter events, 0.2 us)
Async XLA Ops:
  7.2 2049.0 %all-reduce.2.cloned.1.call-start = ((), (), s32[]{:S(2)}) async-start(), calls=%async_computation | async-start | bytes 9289728 | tf_op jit(solution)/shard_map/psum | solution.py:56
  42.4 3.2 copy-start.6
  42.4 3.4 copy-start.3
  45.8 4.3 copy-start
  45.8 2010.4 %copy-start.4 = (s32[81]{0:T(128)S(1)}, s32[81]{0:T(128)}, u32[]{:S(2)}) copy-start(s32[81]{0:T(128)} %param.18) | copy-start | bytes 976
  2061.4 4.2 copy-start.2
  2061.4 4.2 copy-start.5
  2061.4 5.0 copy-start.1
Sparse Core Ops, SparseCore 0:
  50.2 2005.9 all-reduce.1
where the time goes:
time: 2070 us
  waiting for transfers between devices  2010 us (97%)
  blocking collectives  31.3 us (2%)
    psum x1, waiting for transfers between devices, shards(): seq_values = lax.psum(partial_values, 'turn')  2010 us
  transfers between devices with their start and end apart: 1, of which 1 were waited for; matrix products, arithmetic and copies ran while one was open for 0% of the time, Pallas kernels for 0%

commit v1 on v0

v1 whole, which is shorter than its diff:
```python
import jax
import jax.numpy as jnp
from jax import lax
from jax.experimental import pallas as pl
from jax.experimental.pallas import tpu as pltpu
from jax.sharding import PartitionSpec as P

SLOTS = 56
UNITS = 128
PLANE = 16
LINE = 8
VMEM = 48 * 1024 * 1024


def spread(count):
    return [pl.BlockSpec(memory_space=pltpu.VMEM)] * count


def scalars(count):
    return [pl.BlockSpec(memory_space=pltpu.SMEM)] * count


def weigh(pot, turn_act, flop_act, reach, ranks, live, out, acc):
    seqs, boards, width = reach.shape
    acc[...] = jnp.zeros_like(acc)
    half = acc.shape[0] // 2
    for s in range(seqs):
        term = reach[s].astype(jnp.float32) * pot[s]
        acc[turn_act[s]] += term
        acc[half + flop_act[s]] += term
    alive = live[...].astype(jnp.float32)
    for r in range(acc.shape[0]):
        out[pl.ds(r * boards, boards), :] = acc[r] * alive
    top = acc.shape[0] * boards
    out[pl.ds(top, boards), :] = ranks[...].astype(jnp.float32)
    out[pl.ds(top + boards, boards), :] = jnp.zeros((boards, width), jnp.float32)


def showdown(turn_of, payload, ranks, live, cards, out, acc):
    hands, rows, width = payload.shape
    boards = ranks.shape[0]
    actions = acc.shape[0] // (2 * boards)
    me = lax.axis_index("hand")
    used = acc.shape[0]
    here = cards[:, pl.ds(pl.multiple_of(me * width, width), width)].astype(jnp.float32)
    mine = jnp.concatenate(
        [ranks[...].astype(jnp.float32), here, jnp.zeros((2, width), jnp.float32)], axis=0
    )
    columns = jnp.transpose(mine)
    first, second = columns[:, boards : boards + 1], columns[:, boards + 1 : boards + 2]
    row = lax.broadcasted_iota(jnp.int32, (used, 1), 0) % boards
    total = jnp.zeros((used, width), jnp.float32)
    parts = [jnp.zeros((used, width), jnp.float32) for _ in range(boards)]
    for h in range(hands):
        x = payload[h, :used, :]
        high = x.astype(jnp.bfloat16)
        rest = x - high.astype(jnp.float32)
        mid = rest.astype(jnp.bfloat16)
        low = (rest - mid.astype(jnp.float32)).astype(jnp.bfloat16)
        there = cards[:, h * width : (h + 1) * width].astype(jnp.float32)
        one, two = there[0:1], there[1:2]
        shared = (first == one) | (first == two) | (second == one) | (second == two)
        apart = jnp.where(shared, 0.0, 1.0)
        for b in range(boards):
            theirs = payload[h, used + b : used + b + 1, :]
            sign = jnp.clip(columns[:, b : b + 1] - theirs, -1.0, 1.0)
            tile = (sign * apart).astype(jnp.bfloat16)
            for piece in (low, mid, high):
                parts[b] += lax.dot_general(
                    piece, tile, (((1,), (1,)), ((), ())), preferred_element_type=jnp.float32
                )
    for b in range(boards):
        alive = live[b : b + 1, :].astype(jnp.float32)
        total += jnp.where(row == b, parts[b], 0.0) * alive
    acc[...] = total
    slot = lax.broadcasted_iota(jnp.int32, (SLOTS, 128), 0)
    turns = 49
    hits = [(slot == turn_of[b]).astype(jnp.float32) for b in range(boards)]
    flop = (slot == turns).astype(jnp.float32)
    for a in range(actions):
        for half in range(width // 128):
            lanes = pl.ds(half * 128, 128)
            block = jnp.zeros((SLOTS, 128), jnp.float32)
            ends = jnp.zeros((1, 128), jnp.float32)
            for b in range(boards):
                block += hits[b] * acc[a * boards + b : a * boards + b + 1, lanes]
                at = (actions + a) * boards + b
                ends += acc[at : at + 1, lanes]
            block += flop * ends
            out[pl.ds((a * (width // 128) + half) * SLOTS, SLOTS), :] = block
    filled = actions * (width // 128) * SLOTS
    out[pl.ds(filled, UNITS * 8 - filled), :] = jnp.zeros((UNITS * 8 - filled, 128), jnp.float32)


def add_up(blocks, out):
    total = blocks[0]
    for k in range(1, blocks.shape[0]):
        total += blocks[k]
    for k in range(out.shape[0]):
        out[k] = total


def settle(turns_over_boards, over_boards, sums, turn_regret, flop_regret, turn_out, flop_out, values):
    actions, turns, width = turn_regret.shape
    halves = width // 128
    for half in range(halves):
        lanes = pl.ds(half * 128, 128)
        weighted = jnp.zeros((turns, 128), jnp.float32)
        weight = jnp.zeros((turns, 128), jnp.float32)
        top = jnp.zeros((1, 128), jnp.float32)
        bottom = jnp.zeros((1, 128), jnp.float32)
        for a in range(actions):
            base = (a * halves + half) * SLOTS
            regret = turn_regret[a, :, lanes]
            weighted += regret * (sums[pl.ds(base, turns), :] * turns_over_boards)
            weight += regret
            early = flop_regret[a : a + 1, lanes]
            top += early * (sums[pl.ds(base + turns, 1), :] * over_boards)
            bottom += early
        value = weighted / weight
        values[:, lanes] = value
        root = top / bottom
        for a in range(actions):
            base = (a * halves + half) * SLOTS
            q = sums[pl.ds(base, turns), :] * turns_over_boards
            turn_out[a, :, lanes] = jnp.maximum(turn_regret[a, :, lanes] + q - value, 0.0)
            q = sums[pl.ds(base + turns, 1), :] * over_boards
            flop_out[a : a + 1, lanes] = jnp.maximum(flop_regret[a : a + 1, lanes] + q - root, 0.0)


def shards(
    reach, ranks, live, turn_of, hand_cards, pot, turn_act, flop_act, turn_regret, flop_regret
):
    boards, _, width = reach.shape
    total_hands = hand_cards.shape[1]
    turns, actions, _ = turn_regret.shape
    rows = 2 * actions * boards
    boards_all = boards * lax.axis_size("turn")
    params = pltpu.CompilerParams(vmem_limit_bytes=VMEM)
    f32 = jnp.float32

    payload = pl.pallas_call(
        weigh,
        out_shape=jax.ShapeDtypeStruct((rows + 2 * boards, width), f32),
        in_specs=scalars(3) + spread(3),
        out_specs=pl.BlockSpec(memory_space=pltpu.VMEM),
        scratch_shapes=[pltpu.VMEM((2 * actions, boards, width), f32)],
        compiler_params=params,
    )(pot, turn_act, flop_act, jnp.transpose(reach, (1, 0, 2)), ranks, live)

    gathered = lax.all_gather(payload, "hand", axis=0, tiled=False)

    sums = pl.pallas_call(
        showdown,
        out_shape=jax.ShapeDtypeStruct((UNITS * 8, 128), f32),
        in_specs=scalars(1) + spread(4),
        out_specs=pl.BlockSpec(memory_space=pltpu.VMEM),
        scratch_shapes=[pltpu.VMEM((rows, width), f32)],
        compiler_params=params,
    )(turn_of, gathered, ranks, live, hand_cards)

    chunk = UNITS * 8 // PLANE
    planes = [[k * LINE + z for k in range(PLANE)] for z in range(LINE)]
    lines = [[k * LINE + z for z in range(LINE)] for k in range(PLANE)]

    def copies(blocks, count):
        return pl.pallas_call(
            add_up,
            out_shape=jax.ShapeDtypeStruct((count, chunk, 128), f32),
            in_specs=spread(1),
            out_specs=pl.BlockSpec(memory_space=pltpu.VMEM),
            compiler_params=params,
        )(blocks)

    def swap(blocks, groups):
        return lax.all_to_all(blocks, "turn", 0, 0, axis_index_groups=groups, tiled=True)

    blocks = swap(sums.reshape(PLANE, chunk, 128), planes)
    blocks = swap(copies(blocks, LINE), lines)
    blocks = swap(copies(blocks, PLANE), planes)

    def last(*refs):
        settle(
            turns / boards_all / total_hands, 1.0 / boards_all / total_hands, *refs
        )

    turn_out, flop_out, values = pl.pallas_call(
        last,
        out_shape=(
            jax.ShapeDtypeStruct((actions, turns, width), f32),
            jax.ShapeDtypeStruct((actions, width), f32),
            jax.ShapeDtypeStruct((turns, width), f32),
        ),
        in_specs=spread(3),
        out_specs=tuple(spread(3)),
        compiler_params=params,
    )(blocks.reshape(UNITS * 8, 128), jnp.transpose(turn_regret, (1, 0, 2)), flop_regret)
    return (jnp.transpose(turn_out, (1, 0, 2)), flop_out, values)


def solution(mesh):
    return jax.shard_map(
        shards,
        mesh=mesh,
        in_specs=(
            P("turn", None, "hand"),
            P("turn", "hand"),
            P("turn", "hand"),
            P("turn"),
            P(),
            P(),
            P(),
            P(),
            P(None, None, "hand"),
            P(None, "hand"),
        ),
        out_specs=(P(None, None, "hand"), P(None, "hand"), P(None, "hand")),
        check_vma=False,
    )
```

time: 2070 us -> 87.8 us (0.04)
  the two profiles are of different devices: /device:TPU:0 before, /device:TPU:32 now
where the time goes in v1:
time: 87.8 us; the launch traced here: 87.5 us
  blocking collectives  77.8 us (89%)
  Pallas kernels  5.37 us (6%)
  local copies, waits for them, and re-layouts  3.63 us (4%)
    all_to_all x3, blocking collectives, swap(): lax.all_to_all(blocks, 'turn', 0, 0, axis_index_groups=groups, tiled=True)  58.2 us
    all_gather x1, blocking collectives, shards(): gathered = lax.all_gather(payload, 'hand', axis=0, tiled=False)  19.5 us
    unnamed x24, local copies, waits for them, and re-layouts  3.63 us
    pallas_call x1, Pallas kernels, shards(): pl.pallas_call(showdown, out_shape=jax.ShapeDtypeStruct((UNITS * 8, 128),...  3.02 us

profile of v1, /device:TPU:32, one launch (start us, length us, event | category | flops | bytes accessed | tf_op | source)
XLA Modules:
  0.0 87.5 jit_solution(8043237160562044859)
XLA Ops:
  0.6 0.0 copy-start.10
  0.6 0.0 copy-start.9
  0.7 0.0 copy-start.8
  0.7 0.6 copy-done.10
  1.3 0.0 copy-done.9
  1.3 0.0 copy-done.8
  1.3 0.0 copy-start.1
  1.3 0.9 %copy-done.1 = bf16[4,81,256]{2,0,1:T(4,128)(2,1)S(1)} copy-done((bf16[4,81,256]{2,0,1:T(4,128)(2,1)S(1)}, bf16[4,81,256]{2,0,1:T(4,128)(2,1)}, u32[]{:S(2)}) %copy-start.1) | copy-done | bytes 165912
  2.2 0.0 copy-start.3
  2.2 0.7 copy-done.3
  2.9 0.0 copy-start.5
  2.9 0.7 copy-done.5
  3.6 1.3 %shard_map.121 = f32[80,256]{1,0:T(8,128)S(1)} custom-call(f32[81]{0:T(128)S(1)} %copy-done.8, s32[81]{0:T(128)S(1)} %copy-done.9, s32[81]{0:T(128)S(1)} %copy-done.10, bf16[81,4,256]{2,1,0:T(4,128)(2,1)S(1)} %bitcast.10, s32[4,256]{1,0:T(4,128)S(1)} %copy-done.3, s32[4,256]{1,0:T(4,128)S(1)} %copy-done.5), custom_call_target="tpu_custom_call" | custom-call | tf_op jit(solution)/shard_map/pallas_call | solution.py:142
  4.9 0.0 copy-start.4
  4.9 0.0 copy-start.6
  4.9 0.0 copy-start.7
  5.0 19.5 %all-gather = f32[320,256]{1,0:T(8,128)S(1)} all-gather(f32[80,256]{1,0:T(8,128)S(1)} %shard_map.121), channel_id=2, replica_groups=mesh['turn'=128,'hand'=4] {'hand'}, dimensions={0}, use_global_device_ids=true | all-gather | bytes 409600 | tf_op jit(solution)/shard_map/all_gather | solution.py:151
  24.5 0.0 copy-start.11
  24.5 0.0 copy-done.4
  24.5 0.0 copy-done.6
  24.5 0.0 copy-done.7
  24.5 0.6 copy-done.11
  25.1 3.0 %shard_map.122 = f32[1024,128]{1,0:T(8,128)S(1)} custom-call(s32[4]{0:T(128)S(1)} %copy-done.11, f32[4,80,256]{2,1,0:T(8,128)S(1)} %bitcast.8, s32[4,256]{1,0:T(4,128)S(1)} %copy-done.4, s32[4,256]{1,0:T(4,128)S(1)} %copy-done.6, s32[2,1024]{1,0:T(2,128)S(1)} %copy-done.7), custom_call_target="tpu_custom_call" | custom-call | tf_op jit(solution)/shard_map/pallas_call | solution.py:153
  28.2 18.9 %all_to_all.15.blocks = f32[16,64,128]{2,1,0:T(8,128)S(1)} all-to-all(f32[16,64,128]{2,1,0:T(8,128)S(1)} %bitcast.7), channel_id=1, replica_groups={{0,32,64,96,128,160,192,224,256,288,320,352,384,416,448,480},{4,36,68,1..., dimensions={0} | all-to-all | bytes 1048576 | tf_op jit(solution)/shard_map/all_to_all | solution.py:176
  47.1 25.7 %all_to_all.16.blocks = f32[8,64,128]{2,1,0:T(8,128)S(1)} all-to-all(f32[8,64,128]{2,1,0:T(8,128)S(1)} %shard_map.123), channel_id=1, replica_groups={{0,4,8,12,16,20,24,28},{32,36,40,44,48,52,56,60},{64,68,72,76,80,84,88,..., dimensions={0} | all-to-all | bytes 524288 | tf_op jit(solution)/shard_map/all_to_all | solution.py:176
  72.8 0.1 shard_map.124
  72.9 0.0 copy-start
  72.9 0.0 copy-start.2
  72.9 13.6 %all_to_all.17 = f32[16,64,128]{2,1,0:T(8,128)S(1)} all-to-all(f32[16,64,128]{2,1,0:T(8,128)S(1)} %shard_map.124), channel_id=1, replica_groups={{0,32,64,96,128,160,192,224,256,288,320,352,384,416,448,480},{4,36,68,1..., dimensions={0} | all-to-all | bytes 1048576 | tf_op jit(solution)/shard_map/all_to_all | solution.py:176
  86.5 0.0 copy-done
  86.5 0.0 copy-done.2
  86.5 1.0 %shard_map.125 = (f32[9,49,256]{2,1,0:T(8,128)}, f32[9,256]{1,0:T(8,128)}, f32[49,256]{1,0:T(8,128)}) custom-call(f32[1024,128]{1,0:T(8,128)S(1)} %bitcast.6, f32[9,49,256]{2,1,0:T(8,128)S(1)} %bitcast.9, f32[9,256]{1,0:T(8,128)S(1)} %copy-done.2), custom_call_target="tpu_custom_call" | custom-call | tf_op jit(solution)/shard_map/pallas_call | solution.py:187
  (1 shorter events, 0.0 us)
Async XLA Ops:
  0.6 0.7 copy-start.10
  0.6 0.7 copy-start.9
  0.7 0.7 copy-start.8
  1.3 0.9 %copy-start.1 = (bf16[4,81,256]{2,0,1:T(4,128)(2,1)S(1)}, bf16[4,81,256]{2,0,1:T(4,128)(2,1)}, u32[]{:S(2)}) copy-start(bf16[4,81,256]{2,0,1:T(4,128)(2,1)} %param.10) | copy-start | bytes 497668
  2.2 0.7 copy-start.3
  2.9 0.7 copy-start.5
  4.9 19.6 %copy-start.4 = (s32[4,256]{1,0:T(4,128)S(1)}, s32[4,256]{1,0:T(4,128)}, u32[]{:S(2)}) copy-start(s32[4,256]{1,0:T(4,128)} %ranks.3) | copy-start | bytes 12292
  4.9 19.6 %copy-start.6 = (s32[4,256]{1,0:T(4,128)S(1)}, s32[4,256]{1,0:T(4,128)}, u32[]{:S(2)}) copy-start(s32[4,256]{1,0:T(4,128)} %live.3) | copy-start | bytes 12292
  4.9 19.5 %copy-start.7 = (s32[2,1024]{1,0:T(2,128)S(1)}, s32[2,1024]{1,0:T(2,128)}, u32[]{:S(2)}) copy-start(s32[2,1024]{1,0:T(2,128)} %cards.1) | copy-start | bytes 24580
  24.5 0.7 copy-start.11
  72.9 13.6 %copy-start = (f32[49,9,256]{2,0,1:T(8,128)S(1)}, f32[49,9,256]{2,0,1:T(8,128)}, u32[]{:S(2)}) copy-start(f32[49,9,256]{2,0,1:T(8,128)} %param.18) | copy-start | bytes 1354756
  72.9 13.6 %copy-start.2 = (f32[9,256]{1,0:T(8,128)S(1)}, f32[9,256]{1,0:T(8,128)}, u32[]{:S(2)}) copy-start(f32[9,256]{1,0:T(8,128)} %refs_2_.1) | copy-start | bytes 27652

commit v2 on v1

--- a/solution.py
+++ b/solution.py
@@ -5,24 +5,34 @@
 from jax.experimental.pallas import tpu as pltpu
 from jax.sharding import PartitionSpec as P
 
+TURNS = 49
 SLOTS = 56
 UNITS = 128
 PLANE = 16
 LINE = 8
 VMEM = 48 * 1024 * 1024
+WHOLE = 60 * 1024 * 1024
 
 
 def spread(count):
     return [pl.BlockSpec(memory_space=pltpu.VMEM)] * count
 
 
-def scalars(count):
-    return [pl.BlockSpec(memory_space=pltpu.SMEM)] * count
-
-
-def weigh(pot, turn_act, flop_act, reach, ranks, live, out, acc):
+def weigh(
+    pot_hbm, turn_hbm, flop_hbm, of_hbm, reach_hbm, ranks_hbm, live_hbm, out,
+    acc, pot, turn_act, flop_act, turn_of, reach, ranks, live, sems
+):
+    pairs = (
+        (reach_hbm, reach), (pot_hbm, pot), (turn_hbm, turn_act), (flop_hbm, flop_act),
+        (of_hbm, turn_of), (ranks_hbm, ranks), (live_hbm, live),
+    )
+    moves = [pltpu.make_async_copy(x, y, sems.at[k]) for k, (x, y) in enumerate(pairs)]
+    for move in moves:
+        move.start()
+    acc[...] = jnp.zeros_like(acc)
+    for move in moves:
+        move.wait()
     seqs, boards, width = reach.shape
-    acc[...] = jnp.zeros_like(acc)
     half = acc.shape[0] // 2
     for s in range(seqs):
         term = reach[s].astype(jnp.float32) * pot[s]
@@ -33,30 +43,33 @@
         out[pl.ds(r * boards, boards), :] = acc[r] * alive
     top = acc.shape[0] * boards
     out[pl.ds(top, boards), :] = ranks[...].astype(jnp.float32)
-    out[pl.ds(top + boards, boards), :] = jnp.zeros((boards, width), jnp.float32)
-
-
-def showdown(turn_of, payload, ranks, live, cards, out, acc):
+    for b in range(boards):
+        out[pl.ds(top + boards + b, 1), :] = jnp.full((1, width), turn_of[b], jnp.int32).astype(
+            jnp.float32
+        )
+
+
+def showdown(payload, ranks, live, cards, out, acc):
     hands, rows, width = payload.shape
     boards = ranks.shape[0]
-    actions = acc.shape[0] // (2 * boards)
+    used = rows - 2 * boards
+    actions = used // (2 * boards)
     me = lax.axis_index("hand")
-    used = acc.shape[0]
     here = cards[:, pl.ds(pl.multiple_of(me * width, width), width)].astype(jnp.float32)
     mine = jnp.concatenate(
         [ranks[...].astype(jnp.float32), here, jnp.zeros((2, width), jnp.float32)], axis=0
     )
     columns = jnp.transpose(mine)
     first, second = columns[:, boards : boards + 1], columns[:, boards + 1 : boards + 2]
-    row = lax.broadcasted_iota(jnp.int32, (used, 1), 0) % boards
-    total = jnp.zeros((used, width), jnp.float32)
-    parts = [jnp.zeros((used, width), jnp.float32) for _ in range(boards)]
+    row = lax.broadcasted_iota(jnp.int32, (rows, 1), 0) % boards
+    parts = [jnp.zeros((3 * rows, width), jnp.float32) for _ in range(boards)]
     for h in range(hands):
-        x = payload[h, :used, :]
+        x = payload[h]
         high = x.astype(jnp.bfloat16)
         rest = x - high.astype(jnp.float32)
         mid = rest.astype(jnp.bfloat16)
         low = (rest - mid.astype(jnp.float32)).astype(jnp.bfloat16)
+        pieces = jnp.concatenate([high, mid, low], axis=0)
         there = cards[:, h * width : (h + 1) * width].astype(jnp.float32)
         one, two = there[0:1], there[1:2]
         shared = (first == one) | (first == two) | (second == one) | (second == two)
@@ -65,18 +78,23 @@
             theirs = payload[h, used + b : used + b + 1, :]
             sign = jnp.clip(columns[:, b : b + 1] - theirs, -1.0, 1.0)
             tile = (sign * apart).astype(jnp.bfloat16)
-            for piece in (low, mid, high):
-                parts[b] += lax.dot_general(
-                    piece, tile, (((1,), (1,)), ((), ())), preferred_element_type=jnp.float32
-                )
+            parts[b] += lax.dot_general(
+                pieces, tile, (((1,), (1,)), ((), ())), preferred_element_type=jnp.float32
+            )
+    total = jnp.zeros((rows, width), jnp.float32)
     for b in range(boards):
         alive = live[b : b + 1, :].astype(jnp.float32)
-        total += jnp.where(row == b, parts[b], 0.0) * alive
+        part = parts[b][:rows] + (parts[b][rows : 2 * rows] + parts[b][2 * rows :])
+        total += jnp.where(row == b, part, 0.0) * alive
     acc[...] = total
     slot = lax.broadcasted_iota(jnp.int32, (SLOTS, 128), 0)
-    turns = 49
-    hits = [(slot == turn_of[b]).astype(jnp.float32) for b in range(boards)]
-    flop = (slot == turns).astype(jnp.float32)
+    card = slot.astype(jnp.float32)
+    flop_at = used + boards
+    hits = [
+        (card == payload[0, flop_at + b : flop_at + b + 1, :128]).astype(jnp.float32)
+        for b in range(boards)
+    ]
+    flop = (slot == TURNS).astype(jnp.float32)
     for a in range(actions):
         for half in range(width // 128):
             lanes = pl.ds(half * 128, 128)
@@ -131,7 +149,7 @@
 def shards(
     reach, ranks, live, turn_of, hand_cards, pot, turn_act, flop_act, turn_regret, flop_regret
 ):
-    boards, _, width = reach.shape
+    boards, seqs, width = reach.shape
     total_hands = hand_cards.shape[1]
     turns, actions, _ = turn_regret.shape
     rows = 2 * actions * boards
@@ -142,22 +160,32 @@
     payload = pl.pallas_call(
         weigh,
         out_shape=jax.ShapeDtypeStruct((rows + 2 * boards, width), f32),
-        in_specs=scalars(3) + spread(3),
+        in_specs=[pl.BlockSpec(memory_space=pltpu.HBM)] * 7,
         out_specs=pl.BlockSpec(memory_space=pltpu.VMEM),
-        scratch_shapes=[pltpu.VMEM((2 * actions, boards, width), f32)],
-        compiler_params=params,
-    )(pot, turn_act, flop_act, jnp.transpose(reach, (1, 0, 2)), ranks, live)
+        scratch_shapes=[
+            pltpu.VMEM((2 * actions, boards, width), f32),
+            pltpu.SMEM(pot.shape, f32),
+            pltpu.SMEM(turn_act.shape, jnp.int32),
+            pltpu.SMEM(flop_act.shape, jnp.int32),
+            pltpu.SMEM(turn_of.shape, jnp.int32),
+            pltpu.VMEM((seqs, boards, width), reach.dtype),
+            pltpu.VMEM(ranks.shape, jnp.int32),
+            pltpu.VMEM(live.shape, jnp.int32),
+            pltpu.SemaphoreType.DMA((7,)),
+        ],
+        compiler_params=pltpu.CompilerParams(vmem_limit_bytes=WHOLE),
+    )(pot, turn_act, flop_act, turn_of, jnp.transpose(reach, (1, 0, 2)), ranks, live)
 
     gathered = lax.all_gather(payload, "hand", axis=0, tiled=False)
 
     sums = pl.pallas_call(
         showdown,
         out_shape=jax.ShapeDtypeStruct((UNITS * 8, 128), f32),
-        in_specs=scalars(1) + spread(4),
+        in_specs=spread(4),
         out_specs=pl.BlockSpec(memory_space=pltpu.VMEM),
-        scratch_shapes=[pltpu.VMEM((rows, width), f32)],
+        scratch_shapes=[pltpu.VMEM((rows + 2 * boards, width), f32)],
         compiler_params=params,
-    )(turn_of, gathered, ranks, live, hand_cards)
+    )(gathered, ranks, live, hand_cards)
 
     chunk = UNITS * 8 // PLANE
     planes = [[k * LINE + z for k in range(PLANE)] for z in range(LINE)]

time: 87.8 us -> 83.7 us (0.953)
  local copies, waits for them, and re-layouts: 3.63 us -> 0.03 us
    unnamed x24 -> x10, local copies, waits for them, and re-layouts: 3.63 us -> 0.03 us
    pallas_call x1, Pallas kernels: 3.02 us -> 1.33 us  [shards(): pl.pallas_call(showdown, out_shape=jax.ShapeDtypeStruct((UNITS * 8, 128),...]
    pallas_call x1, Pallas kernels: 1.3 us -> 2.41 us  [shards(): pl.pallas_call(weigh, out_shape=jax.ShapeDtypeStruct((rows + 2 * boards,...]
where the time goes in v2:
time: 83.7 us; the launch traced here: 83.5 us
  blocking collectives  78 us (93%)
  Pallas kernels  4.77 us (6%)
    all_to_all x3, blocking collectives, swap(): lax.all_to_all(blocks, 'turn', 0, 0, axis_index_groups=groups, tiled=True)  58.2 us
    all_gather x1, blocking collectives, shards(): gathered = lax.all_gather(payload, 'hand', axis=0, tiled=False)  19.7 us
    pallas_call x1, Pallas kernels, shards(): pl.pallas_call(weigh, out_shape=jax.ShapeDtypeStruct((rows + 2 * boards,...  2.41 us

profile of v2, /device:TPU:32, one launch (start us, length us, event | category | flops | bytes accessed | tf_op | source)
XLA Modules:
  0.0 83.5 jit_solution(161204709895658234)
XLA Ops:
  0.6 2.4 %shard_map.121 = f32[80,256]{1,0:T(8,128)} custom-call(f32[81]{0:T(128)} %pot_hbm.1, s32[81]{0:T(128)} %turn_hbm.1, s32[81]{0:T(128)} %flop_hbm.1, s32[4]{0:T(128)} %of_hbm.1, bf16[81,4,256]{2,1,0:T(4,128)(2,1)} %bitcast.10, s32[4,256]{1,0:T(4,128)} %ranks.1, s32[4,256]{1,0:T(4,128)} %live.1), custom_call_target="tpu_custom_call" | custom-call | tf_op jit(solution)/shard_map/pallas_call | solution.py:160
  3.0 0.0 copy-start.2
  3.1 0.0 copy-start.3
  3.1 0.0 copy-start.4
  3.1 19.7 %all-gather = f32[320,256]{1,0:T(8,128)S(1)} all-gather(f32[80,256]{1,0:T(8,128)} %shard_map.121), channel_id=2, replica_groups=mesh['turn'=128,'hand'=4] {'hand'}, dimensions={0}, use_global_device_ids=true | all-gather | bytes 409600 | tf_op jit(solution)/shard_map/all_gather | solution.py:179
  22.8 0.0 copy-done.2
  22.8 0.0 copy-done.3
  22.8 0.0 copy-done.4
  22.8 1.3 %shard_map.122 = f32[1024,128]{1,0:T(8,128)S(1)} custom-call(f32[4,80,256]{2,1,0:T(8,128)S(1)} %bitcast.8, s32[4,256]{1,0:T(4,128)S(1)} %copy-done.2, s32[4,256]{1,0:T(4,128)S(1)} %copy-done.3, s32[2,1024]{1,0:T(2,128)S(1)} %copy-done.4), custom_call_target="tpu_custom_call" | custom-call | tf_op jit(solution)/shard_map/pallas_call | solution.py:181
  24.2 18.9 %all_to_all.15.blocks = f32[16,64,128]{2,1,0:T(8,128)S(1)} all-to-all(f32[16,64,128]{2,1,0:T(8,128)S(1)} %bitcast.7), channel_id=1, replica_groups={{0,32,64,96,128,160,192,224,256,288,320,352,384,416,448,480},{4,36,68,1..., dimensions={0} | all-to-all | bytes 1048576 | tf_op jit(solution)/shard_map/all_to_all | solution.py:204
  43.1 25.7 %all_to_all.16.blocks = f32[8,64,128]{2,1,0:T(8,128)S(1)} all-to-all(f32[8,64,128]{2,1,0:T(8,128)S(1)} %shard_map.123), channel_id=1, replica_groups={{0,4,8,12,16,20,24,28},{32,36,40,44,48,52,56,60},{64,68,72,76,80,84,88,..., dimensions={0} | all-to-all | bytes 524288 | tf_op jit(solution)/shard_map/all_to_all | solution.py:204
  68.8 0.1 shard_map.124
  68.9 0.0 copy-start
  68.9 0.0 copy-start.1
  68.9 13.6 %all_to_all.17 = f32[16,64,128]{2,1,0:T(8,128)S(1)} all-to-all(f32[16,64,128]{2,1,0:T(8,128)S(1)} %shard_map.124), channel_id=1, replica_groups={{0,32,64,96,128,160,192,224,256,288,320,352,384,416,448,480},{4,36,68,1..., dimensions={0} | all-to-all | bytes 1048576 | tf_op jit(solution)/shard_map/all_to_all | solution.py:204
  82.5 0.0 copy-done
  82.5 0.0 copy-done.1
  82.5 0.9 %shard_map.125 = (f32[9,49,256]{2,1,0:T(8,128)}, f32[9,256]{1,0:T(8,128)}, f32[49,256]{1,0:T(8,128)}) custom-call(f32[1024,128]{1,0:T(8,128)S(1)} %bitcast.6, f32[9,49,256]{2,1,0:T(8,128)S(1)} %bitcast.9, f32[9,256]{1,0:T(8,128)S(1)} %copy-done.1), custom_call_target="tpu_custom_call" | custom-call | tf_op jit(solution)/shard_map/pallas_call | solution.py:215
  (1 shorter events, 0.0 us)
Async XLA Ops:
  3.0 19.8 %copy-start.2 = (s32[4,256]{1,0:T(4,128)S(1)}, s32[4,256]{1,0:T(4,128)}, u32[]{:S(2)}) copy-start(s32[4,256]{1,0:T(4,128)} %ranks.1) | copy-start | bytes 12292
  3.1 19.8 %copy-start.3 = (s32[4,256]{1,0:T(4,128)S(1)}, s32[4,256]{1,0:T(4,128)}, u32[]{:S(2)}) copy-start(s32[4,256]{1,0:T(4,128)} %live.1) | copy-start | bytes 12292
  3.1 19.8 %copy-start.4 = (s32[2,1024]{1,0:T(2,128)S(1)}, s32[2,1024]{1,0:T(2,128)}, u32[]{:S(2)}) copy-start(s32[2,1024]{1,0:T(2,128)} %cards.1) | copy-start | bytes 24580
  68.9 13.6 %copy-start = (f32[49,9,256]{2,0,1:T(8,128)S(1)}, f32[49,9,256]{2,0,1:T(8,128)}, u32[]{:S(2)}) copy-start(f32[49,9,256]{2,0,1:T(8,128)} %param.18) | copy-start | bytes 1354756
  68.9 13.6 %copy-start.1 = (f32[9,256]{1,0:T(8,128)S(1)}, f32[9,256]{1,0:T(8,128)}, u32[]{:S(2)}) copy-start(f32[9,256]{1,0:T(8,128)} %refs_2_.1) | copy-start | bytes 27652

commit v3 on v2

--- a/solution.py
+++ b/solution.py
@@ -10,12 +10,36 @@
 UNITS = 128
 PLANE = 16
 LINE = 8
+CHUNK = UNITS * 8 // PLANE
+STEPS = 32760.0
 VMEM = 48 * 1024 * 1024
 WHOLE = 60 * 1024 * 1024
 
 
 def spread(count):
     return [pl.BlockSpec(memory_space=pltpu.VMEM)] * count
+
+
+def pack(x, out, k):
+    rows = x.shape[0]
+    lane = lax.broadcasted_iota(jnp.int32, (16, 128), 1) // 32
+    top = jnp.maximum(jnp.max(jnp.abs(x), axis=1, keepdims=True), 1e-30)
+    log = jnp.ceil(jnp.log2(top) * 256.0)
+    codes = jnp.round(x * (STEPS / jnp.exp2(log * (1.0 / 256.0))))
+    out[k, :rows, :] = codes.astype(jnp.int32).astype(jnp.int16)
+    logs = jnp.zeros((16, 128), jnp.float32)
+    for g in range(rows // 16):
+        logs = jnp.where(lane == g, log[16 * g : 16 * g + 16], logs)
+    out[k, rows:, :] = logs.astype(jnp.int32).astype(jnp.int16)
+
+
+def unpack(block):
+    codes = block[:64].astype(jnp.int32).astype(jnp.float32)
+    logs = block[64:].astype(jnp.int32).astype(jnp.float32)
+    scale = jnp.exp2(logs * (1.0 / 256.0)) * (1.0 / STEPS)
+    return jnp.concatenate(
+        [codes[16 * g : 16 * g + 16] * scale[:, 32 * g : 32 * g + 1] for g in range(4)], axis=0
+    )
 
 
 def weigh(
@@ -49,7 +73,7 @@
         )
 
 
-def showdown(payload, ranks, live, cards, out, acc):
+def showdown(payload, ranks, live, cards, out, acc, dense):
     hands, rows, width = payload.shape
     boards = ranks.shape[0]
     used = rows - 2 * boards
@@ -105,20 +129,25 @@
                 at = (actions + a) * boards + b
                 ends += acc[at : at + 1, lanes]
             block += flop * ends
-            out[pl.ds((a * (width // 128) + half) * SLOTS, SLOTS), :] = block
+            dense[pl.ds((a * (width // 128) + half) * SLOTS, SLOTS), :] = block
     filled = actions * (width // 128) * SLOTS
-    out[pl.ds(filled, UNITS * 8 - filled), :] = jnp.zeros((UNITS * 8 - filled, 128), jnp.float32)
+    dense[pl.ds(filled, UNITS * 8 - filled), :] = jnp.zeros((UNITS * 8 - filled, 128), jnp.float32)
+    for k in range(PLANE):
+        pack(dense[pl.ds(k * CHUNK, CHUNK), :], out, k)
 
 
 def add_up(blocks, out):
-    total = blocks[0]
+    total = unpack(blocks[0])
     for k in range(1, blocks.shape[0]):
-        total += blocks[k]
-    for k in range(out.shape[0]):
-        out[k] = total
-
-
-def settle(turns_over_boards, over_boards, sums, turn_regret, flop_regret, turn_out, flop_out, values):
+        total += unpack(blocks[k])
+    pack(total, out, 0)
+    for k in range(1, out.shape[0]):
+        out[k] = out[0]
+
+
+def settle(turns_over_boards, over_boards, blocks, turn_regret, flop_regret, turn_out, flop_out, values, sums):
+    for k in range(PLANE):
+        sums[pl.ds(k * CHUNK, CHUNK), :] = unpack(blocks[k])
     actions, turns, width = turn_regret.shape
     halves = width // 128
     for half in range(halves):
@@ -180,21 +209,23 @@
 
     sums = pl.pallas_call(
         showdown,
-        out_shape=jax.ShapeDtypeStruct((UNITS * 8, 128), f32),
+        out_shape=jax.ShapeDtypeStruct((PLANE, CHUNK + 16, 128), jnp.int16),
         in_specs=spread(4),
         out_specs=pl.BlockSpec(memory_space=pltpu.VMEM),
-        scratch_shapes=[pltpu.VMEM((rows + 2 * boards, width), f32)],
+        scratch_shapes=[
+            pltpu.VMEM((rows + 2 * boards, width), f32),
+            pltpu.VMEM((UNITS * 8, 128), f32),
+        ],
         compiler_params=params,
     )(gathered, ranks, live, hand_cards)
 
-    chunk = UNITS * 8 // PLANE
     planes = [[k * LINE + z for k in range(PLANE)] for z in range(LINE)]
     lines = [[k * LINE + z for z in range(LINE)] for k in range(PLANE)]
 
     def copies(blocks, count):
         return pl.pallas_call(
             add_up,
-            out_shape=jax.ShapeDtypeStruct((count, chunk, 128), f32),
+            out_shape=jax.ShapeDtypeStruct((count, CHUNK + 16, 128), jnp.int16),
             in_specs=spread(1),
             out_specs=pl.BlockSpec(memory_space=pltpu.VMEM),
             compiler_params=params,
@@ -203,7 +234,7 @@
     def swap(blocks, groups):
         return lax.all_to_all(blocks, "turn", 0, 0, axis_index_groups=groups, tiled=True)
 
-    blocks = swap(sums.reshape(PLANE, chunk, 128), planes)
+    blocks = swap(sums, planes)
     blocks = swap(copies(blocks, LINE), lines)
     blocks = swap(copies(blocks, PLANE), planes)
 
@@ -221,8 +252,9 @@
         ),
         in_specs=spread(3),
         out_specs=tuple(spread(3)),
+        scratch_shapes=[pltpu.VMEM((UNITS * 8, 128), f32)],
         compiler_params=params,
-    )(blocks.reshape(UNITS * 8, 128), jnp.transpose(turn_regret, (1, 0, 2)), flop_regret)
+    )(blocks, jnp.transpose(turn_regret, (1, 0, 2)), flop_regret)
     return (jnp.transpose(turn_out, (1, 0, 2)), flop_out, values)
 
 

time: 83.7 us -> 77.4 us (0.925)
  blocking collectives: 78 us -> 70.5 us
  Pallas kernels: 4.77 us -> 5.87 us
    all_to_all x3, blocking collectives: 58.2 us -> 50.8 us  [swap(): lax.all_to_all(blocks, 'turn', 0, 0, axis_index_groups=groups, tiled=True)]
    pallas_call x3, Pallas kernels: 1.42 us -> 2.31 us  [the longest x1 1.59 us: shards(): pl.pallas_call(showdown, out_shape=jax.ShapeDtypeStruct((PLANE, CHUNK + 1...]
where the time goes in v3:
time: 77.4 us; the launch traced here: 77.1 us
  blocking collectives  70.5 us (91%)
  Pallas kernels  5.87 us (8%)
    all_to_all x3, blocking collectives, swap(): lax.all_to_all(blocks, 'turn', 0, 0, axis_index_groups=groups, tiled=True)  50.8 us
    all_gather x1, blocking collectives, shards(): gathered = lax.all_gather(payload, 'hand', axis=0, tiled=False)  19.7 us
    pallas_call x1, Pallas kernels, shards(): pl.pallas_call(weigh, out_shape=jax.ShapeDtypeStruct((rows + 2 * boards,...  2.41 us
    pallas_call x1, Pallas kernels, shards(): pl.pallas_call(showdown, out_shape=jax.ShapeDtypeStruct((PLANE, CHUNK + 1...  1.59 us

profile of v3, /device:TPU:32, one launch (start us, length us, event | category | flops | bytes accessed | tf_op | source)
XLA Modules:
  0.0 77.1 jit_solution(11964728721872905374)
XLA Ops:
  0.6 2.4 %shard_map.121 = f32[80,256]{1,0:T(8,128)} custom-call(f32[81]{0:T(128)} %pot_hbm.1, s32[81]{0:T(128)} %turn_hbm.1, s32[81]{0:T(128)} %flop_hbm.1, s32[4]{0:T(128)} %of_hbm.1, bf16[81,4,256]{2,1,0:T(4,128)(2,1)} %bitcast.6, s32[4,256]{1,0:T(4,128)} %ranks.1, s32[4,256]{1,0:T(4,128)} %live.1), custom_call_target="tpu_custom_call" | custom-call | tf_op jit(solution)/shard_map/pallas_call | solution.py:189
  3.0 0.0 copy-start.1
  3.1 0.0 copy-start.2
  3.1 0.0 copy-start.4
  3.1 19.7 %all-gather = f32[320,256]{1,0:T(8,128)S(1)} all-gather(f32[80,256]{1,0:T(8,128)} %shard_map.121), channel_id=2, replica_groups=mesh['turn'=128,'hand'=4] {'hand'}, dimensions={0}, use_global_device_ids=true | all-gather | bytes 409600 | tf_op jit(solution)/shard_map/all_gather | solution.py:208
  22.8 0.0 copy-done.1
  22.8 0.0 copy-done.2
  22.8 0.0 copy-done.4
  22.8 1.6 %shard_map.122 = s16[16,80,128]{2,1,0:T(8,128)(2,1)S(1)} custom-call(f32[4,80,256]{2,1,0:T(8,128)S(1)} %bitcast.4, s32[4,256]{1,0:T(4,128)S(1)} %copy-done.1, s32[4,256]{1,0:T(4,128)S(1)} %copy-done.2, s32[2,1024]{1,0:T(2,128)S(1)} %copy-done.4), custom_call_target="tpu_custom_call" | custom-call | tf_op jit(solution)/shard_map/pallas_call | solution.py:210
  24.4 16.7 %all_to_all.15.blocks = s16[16,80,128]{2,1,0:T(8,128)(2,1)S(1)} all-to-all(s16[16,80,128]{2,1,0:T(8,128)(2,1)S(1)} %shard_map.122), channel_id=1, replica_groups={{0,32,64,96,128,160,192,224,256,288,320,352,384,416,448,480},{4,36,68,1..., dimensions={0} | all-to-all | bytes 655360 | tf_op jit(solution)/shard_map/all_to_all | solution.py:235
  41.2 0.4 shard_map.123
  41.6 22.1 %all_to_all.16.blocks = s16[8,80,128]{2,1,0:T(8,128)(2,1)S(1)} all-to-all(s16[8,80,128]{2,1,0:T(8,128)(2,1)S(1)} %shard_map.123), channel_id=1, replica_groups={{0,4,8,12,16,20,24,28},{32,36,40,44,48,52,56,60},{64,68,72,76,80,84,88,..., dimensions={0} | all-to-all | bytes 327680 | tf_op jit(solution)/shard_map/all_to_all | solution.py:235
  63.6 0.0 copy-start
  63.6 0.3 shard_map.124
  63.9 0.0 copy-start.3
  64.0 12.0 %all_to_all.17.refs_0_ = s16[16,80,128]{2,1,0:T(8,128)(2,1)S(1)} all-to-all(s16[16,80,128]{2,1,0:T(8,128)(2,1)S(1)} %shard_map.124), channel_id=1, replica_groups={{0,32,64,96,128,160,192,224,256,288,320,352,384,416,448,480},{4,36,68,1..., dimensions={0} | all-to-all | bytes 655360 | tf_op jit(solution)/shard_map/all_to_all | solution.py:235
  75.9 0.0 copy-done
  75.9 0.0 copy-done.3
  75.9 1.2 %shard_map.125 = (f32[9,49,256]{2,1,0:T(8,128)}, f32[9,256]{1,0:T(8,128)}, f32[49,256]{1,0:T(8,128)}) custom-call(s16[16,80,128]{2,1,0:T(8,128)(2,1)S(1)} %all_to_all.17.refs_0_, f32[9,49,256]{2,1,0:T(8,128)S(1)} %bitcast.5, f32[9,256]{1,0:T(8,128)S(1)} %copy-done.3), custom_call_target="tpu_custom_call" | custom-call | tf_op jit(solution)/shard_map/pallas_call | solution.py:246
Async XLA Ops:
  3.0 19.8 %copy-start.1 = (s32[4,256]{1,0:T(4,128)S(1)}, s32[4,256]{1,0:T(4,128)}, u32[]{:S(2)}) copy-start(s32[4,256]{1,0:T(4,128)} %ranks.1) | copy-start | bytes 12292
  3.1 19.8 %copy-start.2 = (s32[4,256]{1,0:T(4,128)S(1)}, s32[4,256]{1,0:T(4,128)}, u32[]{:S(2)}) copy-start(s32[4,256]{1,0:T(4,128)} %live.1) | copy-start | bytes 12292
  3.1 19.8 %copy-start.4 = (s32[2,1024]{1,0:T(2,128)S(1)}, s32[2,1024]{1,0:T(2,128)}, u32[]{:S(2)}) copy-start(s32[2,1024]{1,0:T(2,128)} %cards.1) | copy-start | bytes 24580
  63.6 12.3 %copy-start = (f32[49,9,256]{2,0,1:T(8,128)S(1)}, f32[49,9,256]{2,0,1:T(8,128)}, u32[]{:S(2)}) copy-start(f32[49,9,256]{2,0,1:T(8,128)} %param.18) | copy-start | bytes 1354756
  63.9 12.0 %copy-start.3 = (f32[9,256]{1,0:T(8,128)S(1)}, f32[9,256]{1,0:T(8,128)}, u32[]{:S(2)}) copy-start(f32[9,256]{1,0:T(8,128)} %refs_2_.1) | copy-start | bytes 27652

commit v4 on v3

--- a/solution.py
+++ b/solution.py
@@ -12,6 +12,7 @@
 LINE = 8
 CHUNK = UNITS * 8 // PLANE
 STEPS = 32760.0
+SCALES = 58
 VMEM = 48 * 1024 * 1024
 WHOLE = 60 * 1024 * 1024
 
@@ -20,26 +21,32 @@
     return [pl.BlockSpec(memory_space=pltpu.VMEM)] * count
 
 
-def pack(x, out, k):
-    rows = x.shape[0]
-    lane = lax.broadcasted_iota(jnp.int32, (16, 128), 1) // 32
+def place(column, tile):
+    columns, tiles = UNITS // (SLOTS // 8), SLOTS // 8
+    if tile == tiles - 1 and column < PLANE:
+        return column * CHUNK + CHUNK - 8
+    spot = column * (tiles - 1) + tile if tile < tiles - 1 else columns * (tiles - 1) + column - PLANE
+    return spot // 7 * CHUNK + spot % 7 * 8
+
+
+def pack(x):
+    row = lax.broadcasted_iota(jnp.int32, x.shape, 0)
+    lane = lax.broadcasted_iota(jnp.int32, x.shape, 1)
     top = jnp.maximum(jnp.max(jnp.abs(x), axis=1, keepdims=True), 1e-30)
     log = jnp.ceil(jnp.log2(top) * 256.0)
     codes = jnp.round(x * (STEPS / jnp.exp2(log * (1.0 / 256.0))))
-    out[k, :rows, :] = codes.astype(jnp.int32).astype(jnp.int16)
-    logs = jnp.zeros((16, 128), jnp.float32)
-    for g in range(rows // 16):
-        logs = jnp.where(lane == g, log[16 * g : 16 * g + 16], logs)
-    out[k, rows:, :] = logs.astype(jnp.int32).astype(jnp.int16)
-
-
-def unpack(block):
-    codes = block[:64].astype(jnp.int32).astype(jnp.float32)
-    logs = block[64:].astype(jnp.int32).astype(jnp.float32)
-    scale = jnp.exp2(logs * (1.0 / 256.0)) * (1.0 / STEPS)
-    return jnp.concatenate(
-        [codes[16 * g : 16 * g + 16] * scale[:, 32 * g : 32 * g + 1] for g in range(4)], axis=0
-    )
+    logs = jnp.sum(jnp.where(row == lane, log, 0.0), axis=0, keepdims=True)
+    return jnp.where(row == SCALES, logs, codes).astype(jnp.int32).astype(jnp.int16)
+
+
+def unpack(blocks):
+    count = blocks.shape[0]
+    ends = [blocks[k, 48:64, :].astype(jnp.int32).astype(jnp.float32) for k in range(count)]
+    logs = jnp.concatenate([end[SCALES - 48 : SCALES - 47] for end in ends], axis=0)
+    scales = jnp.transpose(jnp.exp2(logs * (1.0 / 256.0)) * (1.0 / STEPS))
+    for k in range(count):
+        codes = blocks[k].astype(jnp.int32).astype(jnp.float32)
+        yield codes * scales[:64, k : k + 1]
 
 
 def weigh(
@@ -129,27 +136,37 @@
                 at = (actions + a) * boards + b
                 ends += acc[at : at + 1, lanes]
             block += flop * ends
-            dense[pl.ds((a * (width // 128) + half) * SLOTS, SLOTS), :] = block
-    filled = actions * (width // 128) * SLOTS
-    dense[pl.ds(filled, UNITS * 8 - filled), :] = jnp.zeros((UNITS * 8 - filled, 128), jnp.float32)
+            column = a * (width // 128) + half
+            for tile in range(SLOTS // 8):
+                dense[pl.ds(place(column, tile), 8), :] = block[tile * 8 : tile * 8 + 8]
+    spots = {place(c, t) for c in range(actions * (width // 128)) for t in range(SLOTS // 8)}
+    for spot in sorted(set(range(0, UNITS * 8, 8)) - spots):
+        dense[pl.ds(spot, 8), :] = jnp.zeros((8, 128), jnp.float32)
     for k in range(PLANE):
-        pack(dense[pl.ds(k * CHUNK, CHUNK), :], out, k)
+        out[k] = pack(dense[pl.ds(k * CHUNK, CHUNK), :])
 
 
 def add_up(blocks, out):
-    total = unpack(blocks[0])
-    for k in range(1, blocks.shape[0]):
-        total += unpack(blocks[k])
-    pack(total, out, 0)
-    for k in range(1, out.shape[0]):
-        out[k] = out[0]
+    total = jnp.zeros((CHUNK, 128), jnp.float32)
+    for block in unpack(blocks):
+        total += block
+    row = lax.broadcasted_iota(jnp.int32, total.shape, 0)
+    codes = pack(jnp.where(row == SCALES, 0.0, total))
+    for k in range(out.shape[0]):
+        out[k] = codes
 
 
 def settle(turns_over_boards, over_boards, blocks, turn_regret, flop_regret, turn_out, flop_out, values, sums):
-    for k in range(PLANE):
-        sums[pl.ds(k * CHUNK, CHUNK), :] = unpack(blocks[k])
     actions, turns, width = turn_regret.shape
     halves = width // 128
+    for k, block in enumerate(unpack(blocks)):
+        sums[pl.ds(k * CHUNK, CHUNK), :] = block
+
+    def column(at):
+        tiles = [sums[pl.ds(place(at, tile), 8), :] for tile in range(SLOTS // 8)]
+        whole = jnp.concatenate(tiles, axis=0)
+        return whole[:turns] * turns_over_boards, whole[turns : turns + 1] * over_boards
+
     for half in range(halves):
         lanes = pl.ds(half * 128, 128)
         weighted = jnp.zeros((turns, 128), jnp.float32)
@@ -157,22 +174,21 @@
         top = jnp.zeros((1, 128), jnp.float32)
         bottom = jnp.zeros((1, 128), jnp.float32)
         for a in range(actions):
-            base = (a * halves + half) * SLOTS
+            q, flop_q = column(a * halves + half)
             regret = turn_regret[a, :, lanes]
-            weighted += regret * (sums[pl.ds(base, turns), :] * turns_over_boards)
+            weighted += regret * q
             weight += regret
             early = flop_regret[a : a + 1, lanes]
-            top += early * (sums[pl.ds(base + turns, 1), :] * over_boards)
+            top += early * flop_q
             bottom += early
         value = weighted / weight
         values[:, lanes] = value
         root = top / bottom
         for a in range(actions):
-            base = (a * halves + half) * SLOTS
-            q = sums[pl.ds(base, turns), :] * turns_over_boards
+            q, flop_q = column(a * halves + half)
             turn_out[a, :, lanes] = jnp.maximum(turn_regret[a, :, lanes] + q - value, 0.0)
-            q = sums[pl.ds(base + turns, 1), :] * over_boards
-            flop_out[a : a + 1, lanes] = jnp.maximum(flop_regret[a : a + 1, lanes] + q - root, 0.0)
+            early = flop_regret[a : a + 1, lanes]
+            flop_out[a : a + 1, lanes] = jnp.maximum(early + flop_q - root, 0.0)
 
 
 def shards(
@@ -209,7 +225,7 @@
 
     sums = pl.pallas_call(
         showdown,
-        out_shape=jax.ShapeDtypeStruct((PLANE, CHUNK + 16, 128), jnp.int16),
+        out_shape=jax.ShapeDtypeStruct((PLANE, CHUNK, 128), jnp.int16),
         in_specs=spread(4),
         out_specs=pl.BlockSpec(memory_space=pltpu.VMEM),
         scratch_shapes=[
@@ -225,7 +241,7 @@
     def copies(blocks, count):
         return pl.pallas_call(
             add_up,
-            out_shape=jax.ShapeDtypeStruct((count, CHUNK + 16, 128), jnp.int16),
+            out_shape=jax.ShapeDtypeStruct((count, CHUNK, 128), jnp.int16),
             in_specs=spread(1),
             out_specs=pl.BlockSpec(memory_space=pltpu.VMEM),
             compiler_params=params,

time: 77.4 us -> 75.4 us (0.974)
  blocking collectives: 70.5 us -> 68.4 us
    all_to_all x3, blocking collectives: 50.8 us -> 48.6 us  [swap(): lax.all_to_all(blocks, 'turn', 0, 0, axis_index_groups=groups, tiled=True)]
where the time goes in v4:
time: 75.4 us; the launch traced here: 75.2 us
  blocking collectives  68.4 us (91%)
  Pallas kernels  6.07 us (8%)
    all_to_all x3, blocking collectives, swap(): lax.all_to_all(blocks, 'turn', 0, 0, axis_index_groups=groups, tiled=True)  48.6 us
    all_gather x1, blocking collectives, shards(): gathered = lax.all_gather(payload, 'hand', axis=0, tiled=False)  19.7 us
    pallas_call x1, Pallas kernels, shards(): pl.pallas_call(weigh, out_shape=jax.ShapeDtypeStruct((rows + 2 * boards,...  2.41 us
    pallas_call x1, Pallas kernels, shards(): pl.pallas_call(showdown, out_shape=jax.ShapeDtypeStruct((PLANE, CHUNK, 12...  1.6 us

profile of v4, /device:TPU:32, one launch (start us, length us, event | category | flops | bytes accessed | tf_op | source)
XLA Modules:
  0.0 75.2 jit_solution(12660340966623698606)
XLA Ops:
  0.6 2.4 %shard_map.121 = f32[80,256]{1,0:T(8,128)} custom-call(f32[81]{0:T(128)} %pot_hbm.1, s32[81]{0:T(128)} %turn_hbm.1, s32[81]{0:T(128)} %flop_hbm.1, s32[4]{0:T(128)} %of_hbm.1, bf16[81,4,256]{2,1,0:T(4,128)(2,1)} %bitcast.6, s32[4,256]{1,0:T(4,128)} %ranks.1, s32[4,256]{1,0:T(4,128)} %live.1), custom_call_target="tpu_custom_call" | custom-call | tf_op jit(solution)/shard_map/pallas_call | solution.py:205
  3.0 0.0 copy-start.1
  3.1 0.0 copy-start.2
  3.1 0.0 copy-start.4
  3.1 19.7 %all-gather = f32[320,256]{1,0:T(8,128)S(1)} all-gather(f32[80,256]{1,0:T(8,128)} %shard_map.121), channel_id=2, replica_groups=mesh['turn'=128,'hand'=4] {'hand'}, dimensions={0}, use_global_device_ids=true | all-gather | bytes 409600 | tf_op jit(solution)/shard_map/all_gather | solution.py:224
  22.8 0.0 copy-done.1
  22.8 0.0 copy-done.2
  22.8 0.0 copy-done.4
  22.8 1.6 %shard_map.122 = s16[16,64,128]{2,1,0:T(8,128)(2,1)S(1)} custom-call(f32[4,80,256]{2,1,0:T(8,128)S(1)} %bitcast.4, s32[4,256]{1,0:T(4,128)S(1)} %copy-done.1, s32[4,256]{1,0:T(4,128)S(1)} %copy-done.2, s32[2,1024]{1,0:T(2,128)S(1)} %copy-done.4), custom_call_target="tpu_custom_call" | custom-call | tf_op jit(solution)/shard_map/pallas_call | solution.py:226
  24.4 16.0 %all_to_all.15.blocks = s16[16,64,128]{2,1,0:T(8,128)(2,1)S(1)} all-to-all(s16[16,64,128]{2,1,0:T(8,128)(2,1)S(1)} %shard_map.122), channel_id=1, replica_groups={{0,32,64,96,128,160,192,224,256,288,320,352,384,416,448,480},{4,36,68,1..., dimensions={0} | all-to-all | bytes 524288 | tf_op jit(solution)/shard_map/all_to_all | solution.py:251
  40.5 0.5 shard_map.123
  40.9 20.9 %all_to_all.16.blocks = s16[8,64,128]{2,1,0:T(8,128)(2,1)S(1)} all-to-all(s16[8,64,128]{2,1,0:T(8,128)(2,1)S(1)} %shard_map.123), channel_id=1, replica_groups={{0,4,8,12,16,20,24,28},{32,36,40,44,48,52,56,60},{64,68,72,76,80,84,88,..., dimensions={0} | all-to-all | bytes 262144 | tf_op jit(solution)/shard_map/all_to_all | solution.py:251
  61.9 0.0 copy-start
  61.9 0.4 shard_map.124
  62.3 0.0 copy-start.3
  62.3 11.7 %all_to_all.17.refs_0_ = s16[16,64,128]{2,1,0:T(8,128)(2,1)S(1)} all-to-all(s16[16,64,128]{2,1,0:T(8,128)(2,1)S(1)} %shard_map.124), channel_id=1, replica_groups={{0,32,64,96,128,160,192,224,256,288,320,352,384,416,448,480},{4,36,68,1..., dimensions={0} | all-to-all | bytes 524288 | tf_op jit(solution)/shard_map/all_to_all | solution.py:251
  73.9 0.0 copy-done
  73.9 0.0 copy-done.3
  74.0 1.2 %shard_map.125 = (f32[9,49,256]{2,1,0:T(8,128)}, f32[9,256]{1,0:T(8,128)}, f32[49,256]{1,0:T(8,128)}) custom-call(s16[16,64,128]{2,1,0:T(8,128)(2,1)S(1)} %all_to_all.17.refs_0_, f32[9,49,256]{2,1,0:T(8,128)S(1)} %bitcast.5, f32[9,256]{1,0:T(8,128)S(1)} %copy-done.3), custom_call_target="tpu_custom_call" | custom-call | tf_op jit(solution)/shard_map/pallas_call | solution.py:262
Async XLA Ops:
  3.0 19.8 %copy-start.1 = (s32[4,256]{1,0:T(4,128)S(1)}, s32[4,256]{1,0:T(4,128)}, u32[]{:S(2)}) copy-start(s32[4,256]{1,0:T(4,128)} %ranks.1) | copy-start | bytes 12292
  3.1 19.8 %copy-start.2 = (s32[4,256]{1,0:T(4,128)S(1)}, s32[4,256]{1,0:T(4,128)}, u32[]{:S(2)}) copy-start(s32[4,256]{1,0:T(4,128)} %live.1) | copy-start | bytes 12292
  3.1 19.8 %copy-start.4 = (s32[2,1024]{1,0:T(2,128)S(1)}, s32[2,1024]{1,0:T(2,128)}, u32[]{:S(2)}) copy-start(s32[2,1024]{1,0:T(2,128)} %cards.1) | copy-start | bytes 24580
  61.9 12.1 %copy-start = (f32[49,9,256]{2,0,1:T(8,128)S(1)}, f32[49,9,256]{2,0,1:T(8,128)}, u32[]{:S(2)}) copy-start(f32[49,9,256]{2,0,1:T(8,128)} %param.18) | copy-start | bytes 1354756
  62.3 11.7 %copy-start.3 = (f32[9,256]{1,0:T(8,128)S(1)}, f32[9,256]{1,0:T(8,128)}, u32[]{:S(2)}) copy-start(f32[9,256]{1,0:T(8,128)} %refs_2_.1) | copy-start | bytes 27652

commit v5 on v4

--- a/solution.py
+++ b/solution.py
@@ -14,7 +14,7 @@
 STEPS = 32760.0
 SCALES = 58
 VMEM = 48 * 1024 * 1024
-WHOLE = 60 * 1024 * 1024
+BANKS = 4
 
 
 def spread(count):
@@ -51,7 +51,7 @@
 
 def weigh(
     pot_hbm, turn_hbm, flop_hbm, of_hbm, reach_hbm, ranks_hbm, live_hbm, out,
-    acc, pot, turn_act, flop_act, turn_of, reach, ranks, live, sems
+    pot, turn_act, flop_act, turn_of, reach, ranks, live, sems, *banks
 ):
     pairs = (
         (reach_hbm, reach), (pot_hbm, pot), (turn_hbm, turn_act), (flop_hbm, flop_act),
@@ -60,31 +60,41 @@
     moves = [pltpu.make_async_copy(x, y, sems.at[k]) for k, (x, y) in enumerate(pairs)]
     for move in moves:
         move.start()
-    acc[...] = jnp.zeros_like(acc)
+    turn_sums, flop_sums = banks[:BANKS], banks[BANKS:]
+    for bank in banks:
+        bank[...] = jnp.zeros_like(bank)
     for move in moves:
         move.wait()
     seqs, boards, width = reach.shape
-    half = acc.shape[0] // 2
+    halves = [slice(half * 128, half * 128 + 128) for half in range(width // 128)]
     for s in range(seqs):
         term = reach[s].astype(jnp.float32) * pot[s]
-        acc[turn_act[s]] += term
-        acc[half + flop_act[s]] += term
+        turn_sums[s % BANKS][turn_act[s]] += term
+        flop_sums[s % BANKS][flop_act[s]] += term
     alive = live[...].astype(jnp.float32)
-    for r in range(acc.shape[0]):
-        out[pl.ds(r * boards, boards), :] = acc[r] * alive
-    top = acc.shape[0] * boards
-    out[pl.ds(top, boards), :] = ranks[...].astype(jnp.float32)
-    for b in range(boards):
-        out[pl.ds(top + boards + b, 1), :] = jnp.full((1, width), turn_of[b], jnp.int32).astype(
-            jnp.float32
-        )
-
-
-def showdown(payload, ranks, live, cards, out, acc, dense):
-    hands, rows, width = payload.shape
+    top = 0
+    for sums in (turn_sums, flop_sums):
+        for r in range(sums[0].shape[0]):
+            total = sums[0][r]
+            for other in sums[1:]:
+                total += other[r]
+            total *= alive
+            for half, lanes in enumerate(halves):
+                out[half, pl.ds(top, boards), :] = total[:, lanes]
+            top += boards
+    for half, lanes in enumerate(halves):
+        out[half, pl.ds(top, boards), :] = ranks[:, lanes].astype(jnp.float32)
+        for b in range(boards):
+            card = jnp.full((1, 128), turn_of[b], jnp.int32).astype(jnp.float32)
+            out[half, pl.ds(top + boards + b, 1), :] = card
+
+
+def showdown(payload, ranks, live, cards, out, dense):
+    hands, halves, rows, _ = payload.shape
+    width = halves * 128
     boards = ranks.shape[0]
-    used = rows - 2 * boards
-    actions = used // (2 * boards)
+    each = rows // boards
+    actions = (each - 2) // 2
     me = lax.axis_index("hand")
     here = cards[:, pl.ds(pl.multiple_of(me * width, width), width)].astype(jnp.float32)
     mine = jnp.concatenate(
@@ -92,50 +102,46 @@
     )
     columns = jnp.transpose(mine)
     first, second = columns[:, boards : boards + 1], columns[:, boards + 1 : boards + 2]
-    row = lax.broadcasted_iota(jnp.int32, (rows, 1), 0) % boards
-    parts = [jnp.zeros((3 * rows, width), jnp.float32) for _ in range(boards)]
+    aparts = []
     for h in range(hands):
-        x = payload[h]
-        high = x.astype(jnp.bfloat16)
-        rest = x - high.astype(jnp.float32)
-        mid = rest.astype(jnp.bfloat16)
-        low = (rest - mid.astype(jnp.float32)).astype(jnp.bfloat16)
-        pieces = jnp.concatenate([high, mid, low], axis=0)
         there = cards[:, h * width : (h + 1) * width].astype(jnp.float32)
         one, two = there[0:1], there[1:2]
         shared = (first == one) | (first == two) | (second == one) | (second == two)
-        apart = jnp.where(shared, 0.0, 1.0)
-        for b in range(boards):
-            theirs = payload[h, used + b : used + b + 1, :]
-            sign = jnp.clip(columns[:, b : b + 1] - theirs, -1.0, 1.0)
-            tile = (sign * apart).astype(jnp.bfloat16)
-            parts[b] += lax.dot_general(
-                pieces, tile, (((1,), (1,)), ((), ())), preferred_element_type=jnp.float32
-            )
-    total = jnp.zeros((rows, width), jnp.float32)
-    for b in range(boards):
-        alive = live[b : b + 1, :].astype(jnp.float32)
-        part = parts[b][:rows] + (parts[b][rows : 2 * rows] + parts[b][2 * rows :])
-        total += jnp.where(row == b, part, 0.0) * alive
-    acc[...] = total
+        aparts.append(jnp.where(shared, 0.0, 1.0))
+    apart = jnp.concatenate(aparts, axis=1)
+    tall = -(-each // 8) * 8
+    sums = []
     slot = lax.broadcasted_iota(jnp.int32, (SLOTS, 128), 0)
     card = slot.astype(jnp.float32)
-    flop_at = used + boards
-    hits = [
-        (card == payload[0, flop_at + b : flop_at + b + 1, :128]).astype(jnp.float32)
-        for b in range(boards)
-    ]
+    hits = []
+    for b in range(boards):
+        x = jnp.concatenate(
+            [payload[h, half, pl.ds(b, each, stride=boards), :] for h in range(hands) for half in range(halves)],
+            axis=1,
+        )
+        theirs = x[each - 2 : each - 1]
+        hits.append((card == x[each - 1 : each, :128]).astype(jnp.float32))
+        x = jnp.concatenate([x, jnp.zeros((tall - each, hands * width), jnp.float32)], axis=0)
+        high = x.astype(jnp.bfloat16).astype(jnp.float32)
+        mid = (x - high).astype(jnp.bfloat16).astype(jnp.float32)
+        pieces = jnp.concatenate([high, mid, x - high - mid], axis=0).astype(jnp.bfloat16)
+        sign = jnp.clip(columns[:, b : b + 1] - theirs, -1.0, 1.0)
+        tile = (sign * apart).astype(jnp.bfloat16)
+        part = lax.dot_general(
+            pieces, tile, (((1,), (1,)), ((), ())), preferred_element_type=jnp.float32
+        )
+        part = part[:tall] + (part[tall : 2 * tall] + part[2 * tall :])
+        sums.append(part * live[b : b + 1, :].astype(jnp.float32))
+    flops = sums[0]
+    for b in range(1, boards):
+        flops += sums[b]
     flop = (slot == TURNS).astype(jnp.float32)
     for a in range(actions):
         for half in range(width // 128):
-            lanes = pl.ds(half * 128, 128)
-            block = jnp.zeros((SLOTS, 128), jnp.float32)
-            ends = jnp.zeros((1, 128), jnp.float32)
+            lanes = slice(half * 128, half * 128 + 128)
+            block = flop * flops[actions + a : actions + a + 1, lanes]
             for b in range(boards):
-                block += hits[b] * acc[a * boards + b : a * boards + b + 1, lanes]
-                at = (actions + a) * boards + b
-                ends += acc[at : at + 1, lanes]
-            block += flop * ends
+                block += hits[b] * sums[b][a : a + 1, lanes]
             column = a * (width // 128) + half
             for tile in range(SLOTS // 8):
                 dense[pl.ds(place(column, tile), 8), :] = block[tile * 8 : tile * 8 + 8]
@@ -202,13 +208,13 @@
     params = pltpu.CompilerParams(vmem_limit_bytes=VMEM)
     f32 = jnp.float32
 
+    operands = (pot, turn_act, flop_act, turn_of, jnp.transpose(reach, (1, 0, 2)), ranks, live)
     payload = pl.pallas_call(
         weigh,
-        out_shape=jax.ShapeDtypeStruct((rows + 2 * boards, width), f32),
+        out_shape=jax.ShapeDtypeStruct((width // 128, rows + 2 * boards, 128), f32),
         in_specs=[pl.BlockSpec(memory_space=pltpu.HBM)] * 7,
         out_specs=pl.BlockSpec(memory_space=pltpu.VMEM),
         scratch_shapes=[
-            pltpu.VMEM((2 * actions, boards, width), f32),
             pltpu.SMEM(pot.shape, f32),
             pltpu.SMEM(turn_act.shape, jnp.int32),
             pltpu.SMEM(flop_act.shape, jnp.int32),
@@ -217,9 +223,10 @@
             pltpu.VMEM(ranks.shape, jnp.int32),
             pltpu.VMEM(live.shape, jnp.int32),
             pltpu.SemaphoreType.DMA((7,)),
+            *[pltpu.VMEM((actions, boards, width), f32)] * (2 * BANKS),
         ],
-        compiler_params=pltpu.CompilerParams(vmem_limit_bytes=WHOLE),
-    )(pot, turn_act, flop_act, turn_of, jnp.transpose(reach, (1, 0, 2)), ranks, live)
+        compiler_params=params,
+    )(*[pltpu.with_memory_space_constraint(x, pltpu.HBM) for x in operands])
 
     gathered = lax.all_gather(payload, "hand", axis=0, tiled=False)
 
@@ -229,7 +236,6 @@
         in_specs=spread(4),
         out_specs=pl.BlockSpec(memory_space=pltpu.VMEM),
         scratch_shapes=[
-            pltpu.VMEM((rows + 2 * boards, width), f32),
             pltpu.VMEM((UNITS * 8, 128), f32),
         ],
         compiler_params=params,

time: 75.4 us -> 73.9 us (0.980)
  Pallas kernels: 6.07 us -> 4.77 us
    pallas_call x1, Pallas kernels: 2.41 us -> 1.19 us  [shards(): pl.pallas_call(weigh, out_shape=jax.ShapeDtypeStruct((width // 128, rows...]
where the time goes in v5:
time: 73.9 us; the launch traced here: 73.7 us
  blocking collectives  68.2 us (92%)
  Pallas kernels  4.77 us (6%)
    all_to_all x3, blocking collectives, swap(): lax.all_to_all(blocks, 'turn', 0, 0, axis_index_groups=groups, tiled=True)  48.6 us
    all_gather x1, blocking collectives, shards(): gathered = lax.all_gather(payload, 'hand', axis=0, tiled=False)  19.5 us
    pallas_call x1, Pallas kernels, shards(): pl.pallas_call(showdown, out_shape=jax.ShapeDtypeStruct((PLANE, CHUNK, 12...  1.51 us

profile of v5, /device:TPU:32, one launch (start us, length us, event | category | flops | bytes accessed | tf_op | source)
XLA Modules:
  0.0 73.7 jit_solution(4700491881343701235)
XLA Ops:
  0.6 1.2 %shard_map.121 = f32[2,80,128]{2,1,0:T(8,128)S(1)} custom-call(f32[81]{0:T(128)} %pot_hbm.1, s32[81]{0:T(128)} %turn_hbm.1, s32[81]{0:T(128)} %flop_hbm.1, s32[4]{0:T(128)} %of_hbm.1, bf16[81,4,256]{2,1,0:T(4,128)(2,1)} %bitcast.6, s32[4,256]{1,0:T(4,128)} %ranks.1, s32[4,256]{1,0:T(4,128)} %live.1), custom_call_target="tpu_custom_call" | custom-call | tf_op jit(solution)/shard_map/pallas_call | solution.py:212
  1.8 0.0 copy-start.1
  1.8 0.0 copy-start.2
  1.9 0.0 copy-start.4
  1.9 19.5 %all-gather = f32[8,80,128]{2,1,0:T(8,128)S(1)} all-gather(f32[2,80,128]{2,1,0:T(8,128)S(1)} %shard_map.121), channel_id=2, replica_groups=mesh['turn'=128,'hand'=4] {'hand'}, dimensions={0}, use_global_device_ids=true | all-gather | bytes 409600 | tf_op jit(solution)/shard_map/all_gather | solution.py:231
  21.4 0.0 copy-done.1
  21.4 0.0 copy-done.2
  21.4 0.0 copy-done.4
  21.4 1.5 %shard_map.122 = s16[16,64,128]{2,1,0:T(8,128)(2,1)S(1)} custom-call(f32[4,2,80,128]{3,2,1,0:T(8,128)S(1)} %bitcast.4, s32[4,256]{1,0:T(4,128)S(1)} %copy-done.1, s32[4,256]{1,0:T(4,128)S(1)} %copy-done.2, s32[2,1024]{1,0:T(2,128)S(1)} %copy-done.4), custom_call_target="tpu_custom_call" | custom-call | tf_op jit(solution)/shard_map/pallas_call | solution.py:233
  22.9 16.0 %all_to_all.15.blocks = s16[16,64,128]{2,1,0:T(8,128)(2,1)S(1)} all-to-all(s16[16,64,128]{2,1,0:T(8,128)(2,1)S(1)} %shard_map.122), channel_id=1, replica_groups={{0,32,64,96,128,160,192,224,256,288,320,352,384,416,448,480},{4,36,68,1..., dimensions={0} | all-to-all | bytes 524288 | tf_op jit(solution)/shard_map/all_to_all | solution.py:257
  39.0 0.5 shard_map.123
  39.4 20.9 %all_to_all.16.blocks = s16[8,64,128]{2,1,0:T(8,128)(2,1)S(1)} all-to-all(s16[8,64,128]{2,1,0:T(8,128)(2,1)S(1)} %shard_map.123), channel_id=1, replica_groups={{0,4,8,12,16,20,24,28},{32,36,40,44,48,52,56,60},{64,68,72,76,80,84,88,..., dimensions={0} | all-to-all | bytes 262144 | tf_op jit(solution)/shard_map/all_to_all | solution.py:257
  60.4 0.0 copy-start
  60.4 0.4 shard_map.124
  60.8 0.0 copy-start.3
  60.8 11.7 %all_to_all.17.refs_0_ = s16[16,64,128]{2,1,0:T(8,128)(2,1)S(1)} all-to-all(s16[16,64,128]{2,1,0:T(8,128)(2,1)S(1)} %shard_map.124), channel_id=1, replica_groups={{0,32,64,96,128,160,192,224,256,288,320,352,384,416,448,480},{4,36,68,1..., dimensions={0} | all-to-all | bytes 524288 | tf_op jit(solution)/shard_map/all_to_all | solution.py:257
  72.4 0.0 copy-done
  72.5 0.0 copy-done.3
  72.5 1.2 %shard_map.125 = (f32[9,49,256]{2,1,0:T(8,128)}, f32[9,256]{1,0:T(8,128)}, f32[49,256]{1,0:T(8,128)}) custom-call(s16[16,64,128]{2,1,0:T(8,128)(2,1)S(1)} %all_to_all.17.refs_0_, f32[9,49,256]{2,1,0:T(8,128)S(1)} %bitcast.5, f32[9,256]{1,0:T(8,128)S(1)} %copy-done.3), custom_call_target="tpu_custom_call" | custom-call | tf_op jit(solution)/shard_map/pallas_call | solution.py:268
Async XLA Ops:
  1.8 19.6 %copy-start.1 = (s32[4,256]{1,0:T(4,128)S(1)}, s32[4,256]{1,0:T(4,128)}, u32[]{:S(2)}) copy-start(s32[4,256]{1,0:T(4,128)} %ranks.1) | copy-start | bytes 12292
  1.8 19.6 %copy-start.2 = (s32[4,256]{1,0:T(4,128)S(1)}, s32[4,256]{1,0:T(4,128)}, u32[]{:S(2)}) copy-start(s32[4,256]{1,0:T(4,128)} %live.1) | copy-start | bytes 12292
  1.9 19.5 %copy-start.4 = (s32[2,1024]{1,0:T(2,128)S(1)}, s32[2,1024]{1,0:T(2,128)}, u32[]{:S(2)}) copy-start(s32[2,1024]{1,0:T(2,128)} %cards.1) | copy-start | bytes 24580
  60.4 12.1 %copy-start = (f32[49,9,256]{2,0,1:T(8,128)S(1)}, f32[49,9,256]{2,0,1:T(8,128)}, u32[]{:S(2)}) copy-start(f32[49,9,256]{2,0,1:T(8,128)} %param.18) | copy-start | bytes 1354756
  60.8 11.7 %copy-start.3 = (f32[9,256]{1,0:T(8,128)S(1)}, f32[9,256]{1,0:T(8,128)}, u32[]{:S(2)}) copy-start(f32[9,256]{1,0:T(8,128)} %refs_2_.1) | copy-start | bytes 27652

commit v6 on v5

--- a/solution.py
+++ b/solution.py
@@ -13,6 +13,13 @@
 CHUNK = UNITS * 8 // PLANE
 STEPS = 32760.0
 SCALES = 58
+BOARD_ROWS = 96
+BOARD_SCALES = 90
+PAGE = 8
+FLOPS = 144
+PAGE_SCALES = 162
+PAGE_ROWS = 176
+SPAN = 64
 VMEM = 48 * 1024 * 1024
 BANKS = 4
 
@@ -29,12 +36,16 @@
     return spot // 7 * CHUNK + spot % 7 * 8
 
 
+def encode(x):
+    top = jnp.maximum(jnp.max(jnp.abs(x), axis=1, keepdims=True), 1e-30)
+    log = jnp.ceil(jnp.log2(top) * 256.0)
+    return jnp.round(x * (STEPS / jnp.exp2(log * (1.0 / 256.0)))), log
+
+
 def pack(x):
     row = lax.broadcasted_iota(jnp.int32, x.shape, 0)
     lane = lax.broadcasted_iota(jnp.int32, x.shape, 1)
-    top = jnp.maximum(jnp.max(jnp.abs(x), axis=1, keepdims=True), 1e-30)
-    log = jnp.ceil(jnp.log2(top) * 256.0)
-    codes = jnp.round(x * (STEPS / jnp.exp2(log * (1.0 / 256.0))))
+    codes, log = encode(x)
     logs = jnp.sum(jnp.where(row == lane, log, 0.0), axis=0, keepdims=True)
     return jnp.where(row == SCALES, logs, codes).astype(jnp.int32).astype(jnp.int16)
 
@@ -89,12 +100,11 @@
             out[half, pl.ds(top + boards + b, 1), :] = card
 
 
-def showdown(payload, ranks, live, cards, out, dense):
+def board_values(payload, ranks, live, cards):
     hands, halves, rows, _ = payload.shape
     width = halves * 128
     boards = ranks.shape[0]
     each = rows // boards
-    actions = (each - 2) // 2
     me = lax.axis_index("hand")
     here = cards[:, pl.ds(pl.multiple_of(me * width, width), width)].astype(jnp.float32)
     mine = jnp.concatenate(
@@ -110,17 +120,14 @@
         aparts.append(jnp.where(shared, 0.0, 1.0))
     apart = jnp.concatenate(aparts, axis=1)
     tall = -(-each // 8) * 8
-    sums = []
-    slot = lax.broadcasted_iota(jnp.int32, (SLOTS, 128), 0)
-    card = slot.astype(jnp.float32)
-    hits = []
+    sums, turn_cards = [], []
     for b in range(boards):
         x = jnp.concatenate(
             [payload[h, half, pl.ds(b, each, stride=boards), :] for h in range(hands) for half in range(halves)],
             axis=1,
         )
         theirs = x[each - 2 : each - 1]
-        hits.append((card == x[each - 1 : each, :128]).astype(jnp.float32))
+        turn_cards.append(x[each - 1 : each, :128])
         x = jnp.concatenate([x, jnp.zeros((tall - each, hands * width), jnp.float32)], axis=0)
         high = x.astype(jnp.bfloat16).astype(jnp.float32)
         mid = (x - high).astype(jnp.bfloat16).astype(jnp.float32)
@@ -132,16 +139,24 @@
         )
         part = part[:tall] + (part[tall : 2 * tall] + part[2 * tall :])
         sums.append(part * live[b : b + 1, :].astype(jnp.float32))
+    return sums, turn_cards, (each - 2) // 2
+
+
+def showdown_all(payload, ranks, live, cards, out, dense):
+    sums, turn_cards, actions = board_values(payload, ranks, live, cards)
+    width = sums[0].shape[1]
     flops = sums[0]
-    for b in range(1, boards):
-        flops += sums[b]
+    for part in sums[1:]:
+        flops += part
+    slot = lax.broadcasted_iota(jnp.int32, (SLOTS, 128), 0)
+    hits = [(slot.astype(jnp.float32) == card).astype(jnp.float32) for card in turn_cards]
     flop = (slot == TURNS).astype(jnp.float32)
     for a in range(actions):
         for half in range(width // 128):
             lanes = slice(half * 128, half * 128 + 128)
             block = flop * flops[actions + a : actions + a + 1, lanes]
-            for b in range(boards):
-                block += hits[b] * sums[b][a : a + 1, lanes]
+            for hit, part in zip(hits, sums):
+                block += hit * part[a : a + 1, lanes]
             column = a * (width // 128) + half
             for tile in range(SLOTS // 8):
                 dense[pl.ds(place(column, tile), 8), :] = block[tile * 8 : tile * 8 + 8]
@@ -150,6 +165,127 @@
         dense[pl.ds(spot, 8), :] = jnp.zeros((8, 128), jnp.float32)
     for k in range(PLANE):
         out[k] = pack(dense[pl.ds(k * CHUNK, CHUNK), :])
+
+
+def showdown(payload, ranks, live, cards, out, rows):
+    sums, turn_cards, actions = board_values(payload, ranks, live, cards)
+    halves = sums[0].shape[1] // 128
+    flops = sums[0]
+    for part in sums[1:]:
+        flops += part
+    rows[...] = jnp.zeros_like(rows)
+    for b, part in enumerate(sums):
+        for half in range(halves):
+            lanes = slice(half * 128, half * 128 + 128)
+            rows[pl.ds((b * halves + half) * actions, actions), :] = part[:actions, lanes]
+    for half in range(halves):
+        lanes = slice(half * 128, half * 128 + 128)
+        at = (len(sums) * halves + half) * actions
+        rows[pl.ds(at, actions), :] = flops[actions : 2 * actions, lanes]
+    x = rows[...]
+    row = lax.broadcasted_iota(jnp.int32, x.shape, 0)
+    lane = lax.broadcasted_iota(jnp.int32, x.shape, 1)
+    codes, log = encode(x)
+    logs = jnp.sum(jnp.where(row == lane, log, 0.0), axis=0, keepdims=True)
+    ids = jnp.zeros((1, 128), jnp.float32)
+    for b, card in enumerate(turn_cards):
+        ids = jnp.where(lane[:1] == b, card, ids)
+    codes = jnp.where(row == BOARD_SCALES, logs, codes)
+    codes = jnp.where(row == BOARD_SCALES + 1, ids, codes)
+    codes = codes.astype(jnp.int32).astype(jnp.int16)
+    for k in range(out.shape[0]):
+        out[k] = codes
+
+
+def run_sums(blocks, out, rows, page):
+    count = blocks.shape[0]
+    boards, halves, actions = 4, 2, 9
+    tails = [blocks[k, 80:96, :].astype(jnp.int32).astype(jnp.float32) for k in range(count)]
+    at = BOARD_SCALES - 80
+    logs = jnp.concatenate([tail[at : at + 1] for tail in tails], axis=0)
+    scales = jnp.transpose(jnp.exp2(logs * (1.0 / 256.0)) * (1.0 / STEPS))
+    for k in range(count):
+        codes = blocks[k].astype(jnp.int32).astype(jnp.float32)
+        rows[k] = codes * scales[:96, k : k + 1]
+    ids = [tail[at + 1 : at + 2] for tail in tails]
+    least = ids[0][:, 0:1]
+    most = ids[-1][:, boards - 1 : boards]
+    slot = lax.broadcasted_iota(jnp.int32, (PAGE, 128), 0).astype(jnp.float32)
+    hits = [
+        [(slot == ids[k][:, b : b + 1] - least).astype(jnp.float32) for b in range(boards)]
+        for k in range(count)
+    ]
+    page[...] = jnp.zeros_like(page)
+    for a in range(actions):
+        for half in range(halves):
+            block = jnp.zeros((PAGE, 128), jnp.float32)
+            for k in range(count):
+                for b in range(boards):
+                    block += hits[k][b] * rows[k, pl.ds((b * halves + half) * actions + a, 1), :]
+            page[pl.ds((a * halves + half) * PAGE, PAGE), :] = block
+    top, flops = boards * halves * actions, halves * actions
+    total = rows[0, pl.ds(top, flops), :]
+    for k in range(1, count):
+        total += rows[k, pl.ds(top, flops), :]
+    page[pl.ds(FLOPS, flops), :] = total
+    x = page[...]
+    row = lax.broadcasted_iota(jnp.int32, x.shape, 0)
+    lane = lax.broadcasted_iota(jnp.int32, x.shape, 1)
+    codes, log = encode(x)
+    for part in range(2):
+        logs = jnp.sum(jnp.where(row == lane + 128 * part, log, 0.0), axis=0, keepdims=True)
+        codes = jnp.where(row == PAGE_SCALES + part, logs, codes)
+    codes = jnp.where(row == PAGE_SCALES + 2, least, codes)
+    codes = jnp.where(row == PAGE_SCALES + 3, most - least + 1.0, codes)
+    codes = codes.astype(jnp.int32).astype(jnp.int16)
+    for k in range(out.shape[0]):
+        out[k] = codes
+
+
+def finish(turns_over_boards, over_boards, blocks, turn_regret, flop_regret, turn_out, flop_out, values, cards, dense):
+    actions, turns, width = turn_regret.shape
+    halves, count = width // 128, blocks.shape[0]
+    at = PAGE_SCALES - 160
+    tails = [blocks[k, 160:176, :].astype(jnp.int32).astype(jnp.float32) for k in range(count)]
+    scales = [
+        jnp.transpose(
+            jnp.exp2(jnp.concatenate([tail[at + part : at + part + 1] for tail in tails], axis=0) * (1.0 / 256.0))
+            * (1.0 / STEPS)
+        )
+        for part in range(2)
+    ]
+    held = jnp.concatenate([tail[at + 3 : at + 4] for tail in tails], axis=0)
+    cards[0] = jnp.max(held).astype(jnp.int32)
+    dense[...] = jnp.zeros_like(dense)
+    flops = jnp.zeros((32, 128), jnp.float32)
+    for k in range(count):
+        codes = blocks[k].astype(jnp.int32).astype(jnp.float32)
+        early = codes[:128] * scales[0][:, k : k + 1]
+        late = codes[128:] * scales[1][:48, k : k + 1]
+        flops += late[16:48]
+        least = jnp.max(tails[k][at + 2 : at + 3]).astype(jnp.int32)
+        for column in range(actions * halves):
+            start = column * PAGE
+            tile = early[start : start + PAGE] if start < 128 else late[start - 128 : start - 128 + PAGE]
+            dense[pl.ds(column * SPAN + least, PAGE), :] += tile
+    for half in range(halves):
+        lanes = pl.ds(half * 128, 128)
+        weighted = jnp.zeros((turns, 128), jnp.float32)
+        weight = jnp.zeros((turns, 128), jnp.float32)
+        for a in range(actions):
+            q = dense[pl.ds((a * halves + half) * SPAN, turns), :] * turns_over_boards
+            regret = turn_regret[a, :, lanes]
+            weighted += regret * q
+            weight += regret
+        value = weighted / weight
+        values[:, lanes] = value
+        early = flop_regret[:, lanes]
+        flop_q = flops[half * actions : half * actions + actions] * over_boards
+        root = jnp.sum(early * flop_q, axis=0, keepdims=True) / jnp.sum(early, axis=0, keepdims=True)
+        flop_out[:, lanes] = jnp.maximum(early + flop_q - root, 0.0)
+        for a in range(actions):
+            q = dense[pl.ds((a * halves + half) * SPAN, turns), :] * turns_over_boards
+            turn_out[a, :, lanes] = jnp.maximum(turn_regret[a, :, lanes] + q - value, 0.0)
 
 
 def add_up(blocks, out):
@@ -230,53 +366,68 @@
 
     gathered = lax.all_gather(payload, "hand", axis=0, tiled=False)
 
-    sums = pl.pallas_call(
-        showdown,
-        out_shape=jax.ShapeDtypeStruct((PLANE, CHUNK, 128), jnp.int16),
-        in_specs=spread(4),
-        out_specs=pl.BlockSpec(memory_space=pltpu.VMEM),
-        scratch_shapes=[
-            pltpu.VMEM((UNITS * 8, 128), f32),
-        ],
-        compiler_params=params,
-    )(gathered, ranks, live, hand_cards)
-
     planes = [[k * LINE + z for k in range(PLANE)] for z in range(LINE)]
     lines = [[k * LINE + z for z in range(LINE)] for k in range(PLANE)]
-
-    def copies(blocks, count):
+    vmem = pl.BlockSpec(memory_space=pltpu.VMEM)
+    factors = (turns / boards_all / total_hands, 1.0 / boards_all / total_hands)
+    by_action = jnp.transpose(turn_regret, (1, 0, 2))
+    outputs = (
+        jax.ShapeDtypeStruct((actions, turns, width), f32),
+        jax.ShapeDtypeStruct((actions, width), f32),
+        jax.ShapeDtypeStruct((turns, width), f32),
+    )
+
+    def call(kernel, shape, scratch, *args):
         return pl.pallas_call(
-            add_up,
-            out_shape=jax.ShapeDtypeStruct((count, CHUNK, 128), jnp.int16),
-            in_specs=spread(1),
-            out_specs=pl.BlockSpec(memory_space=pltpu.VMEM),
+            kernel,
+            out_shape=jax.ShapeDtypeStruct(shape, jnp.int16),
+            in_specs=spread(len(args)),
+            out_specs=vmem,
+            scratch_shapes=[pltpu.VMEM(dims, f32) for dims in scratch],
             compiler_params=params,
-        )(blocks)
+        )(*args)
 
     def swap(blocks, groups):
         return lax.all_to_all(blocks, "turn", 0, 0, axis_index_groups=groups, tiled=True)
 
-    blocks = swap(sums, planes)
-    blocks = swap(copies(blocks, LINE), lines)
-    blocks = swap(copies(blocks, PLANE), planes)
-
-    def last(*refs):
-        settle(
-            turns / boards_all / total_hands, 1.0 / boards_all / total_hands, *refs
+    blocks = call(
+        showdown, (LINE, BOARD_ROWS, 128), [(BOARD_ROWS, 128)], gathered, ranks, live, hand_cards
+    )
+    blocks = swap(blocks, lines)
+    blocks = call(
+        run_sums, (PLANE, PAGE_ROWS, 128), [(LINE, BOARD_ROWS, 128), (PAGE_ROWS, 128)], blocks
+    )
+    blocks = swap(blocks, planes)
+    turn_out, flop_out, values, cards = pl.pallas_call(
+        lambda *refs: finish(*factors, *refs),
+        out_shape=outputs + (jax.ShapeDtypeStruct((1,), jnp.int32),),
+        in_specs=spread(3),
+        out_specs=tuple(spread(3)) + (pl.BlockSpec(memory_space=pltpu.SMEM),),
+        scratch_shapes=[pltpu.VMEM((actions * (width // 128) * SPAN, 128), f32)],
+        compiler_params=params,
+    )(blocks, by_action, flop_regret)
+
+    def every_card(state):
+        payload = gathered + jnp.where(state[0] > PAGE, 0.0, 1.0)
+        scratch = [(UNITS * 8, 128)]
+        chunks = call(
+            showdown_all, (PLANE, CHUNK, 128), scratch, payload, ranks, live, hand_cards
         )
-
-    turn_out, flop_out, values = pl.pallas_call(
-        last,
-        out_shape=(
-            jax.ShapeDtypeStruct((actions, turns, width), f32),
-            jax.ShapeDtypeStruct((actions, width), f32),
-            jax.ShapeDtypeStruct((turns, width), f32),
-        ),
-        in_specs=spread(3),
-        out_specs=tuple(spread(3)),
-        scratch_shapes=[pltpu.VMEM((UNITS * 8, 128), f32)],
-        compiler_params=params,
-    )(blocks, jnp.transpose(turn_regret, (1, 0, 2)), flop_regret)
+        chunks = swap(chunks, planes)
+        chunks = swap(call(add_up, (LINE, CHUNK, 128), [], chunks), lines)
+        chunks = swap(call(add_up, (PLANE, CHUNK, 128), [], chunks), planes)
+        results = pl.pallas_call(
+            lambda *refs: settle(*factors, *refs),
+            out_shape=outputs,
+            in_specs=spread(3),
+            out_specs=tuple(spread(3)),
+            scratch_shapes=[pltpu.VMEM((UNITS * 8, 128), f32)],
+            compiler_params=params,
+        )(chunks, by_action, flop_regret)
+        return (jnp.int32(0),) + tuple(results)
+
+    state = (cards[0], turn_out, flop_out, values)
+    _, turn_out, flop_out, values = lax.while_loop(lambda s: s[0] > PAGE, every_card, state)
     return (jnp.transpose(turn_out, (1, 0, 2)), flop_out, values)
 
 

time: 73.9 us -> 68.8 us (0.931)
  blocking collectives: 68.2 us -> 62.2 us
    all_to_all x3 -> x2, blocking collectives: 48.6 us -> 42.6 us  [swap(): lax.all_to_all(blocks, 'turn', 0, 0, axis_index_groups=groups, tiled=True)]
    pallas_call x4 -> x3, Pallas kernels: 3.58 us -> 3.82 us  [the longest x1 1.91 us: shards(): pl.pallas_call(lambda *refs: finish(*factors, *refs), out_shape=outputs +...]
where the time goes in v6:
time: 68.8 us; the launch traced here: 68.6 us
  blocking collectives  62.2 us (90%)
  Pallas kernels  5.01 us (7%)
  between operations  0.71 us (1%)
    all_to_all x2, blocking collectives, swap(): lax.all_to_all(blocks, 'turn', 0, 0, axis_index_groups=groups, tiled=True)  42.6 us
    all_gather x1, blocking collectives, shards(): gathered = lax.all_gather(payload, 'hand', axis=0, tiled=False)  19.5 us
    pallas_call x1, Pallas kernels, shards(): pl.pallas_call(lambda *refs: finish(*factors, *refs), out_shape=outputs +...  1.91 us
    pallas_call x2, Pallas kernels, call(): pl.pallas_call(kernel, out_shape=jax.ShapeDtypeStruct(shape, jnp.int16),...  1.91 us

profile of v6, /device:TPU:32, one launch (start us, length us, event | category | flops | bytes accessed | tf_op | source)
XLA Modules:
  0.0 68.6 jit_solution(5507714395202316717)
XLA Ops:
  0.6 1.2 %shard_map.121 = f32[2,80,128]{2,1,0:T(8,128)S(1)} custom-call(f32[81]{0:T(128)} %pot_hbm.1, s32[81]{0:T(128)} %turn_hbm.1, s32[81]{0:T(128)} %flop_hbm.1, s32[4]{0:T(128)} %of_hbm.1, bf16[81,4,256]{2,1,0:T(4,128)(2,1)} %bitcast.9, s32[4,256]{1,0:T(4,128)} %ranks.1, s32[4,256]{1,0:T(4,128)} %live.1), custom_call_target="tpu_custom_call" | custom-call | tf_op jit(solution)/shard_map/pallas_call | solution.py:348
  1.8 0.0 copy-start.2
  1.8 0.0 copy-start.3
  1.9 0.0 copy-start.4
  1.9 19.5 %all-gather = f32[8,80,128]{2,1,0:T(8,128)S(1)} all-gather(f32[2,80,128]{2,1,0:T(8,128)S(1)} %shard_map.121), channel_id=2, replica_groups=mesh['turn'=128,'hand'=4] {'hand'}, dimensions={0}, use_global_device_ids=true | all-gather | bytes 409600 | tf_op jit(solution)/shard_map/all_gather | solution.py:367
  21.4 0.0 copy-done.2
  21.4 0.0 copy-done.3
  21.4 0.0 copy-done.4
  21.4 1.2 %shard_map.122 = s16[8,96,128]{2,1,0:T(8,128)(2,1)S(1)} custom-call(f32[4,2,80,128]{3,2,1,0:T(8,128)S(1)} %bitcast.7, s32[4,256]{1,0:T(4,128)S(1)} %copy-done.3, s32[4,256]{1,0:T(4,128)S(1)} %copy-done.4, s32[2,1024]{1,0:T(2,128)S(1)} %copy-done.2), custom_call_target="tpu_custom_call" | custom-call | tf_op jit(solution)/shard_map/pallas_call | solution.py:381
  22.6 24.5 %all_to_all.24.blocks = s16[8,96,128]{2,1,0:T(8,128)(2,1)S(1)} all-to-all(s16[8,96,128]{2,1,0:T(8,128)(2,1)S(1)} %shard_map.122), channel_id=1, replica_groups={{0,4,8,12,16,20,24,28},{32,36,40,44,48,52,56,60},{64,68,72,76,80,84,88,..., dimensions={0} | all-to-all | bytes 393216 | tf_op jit(solution)/shard_map/all_to_all | solution.py:391
  47.1 0.7 shard_map.123
  47.8 0.0 copy-start
  47.8 0.0 copy-start.1
  47.8 18.2 %all_to_all.25.refs_0_ = s16[16,176,128]{2,1,0:T(8,128)(2,1)S(1)} all-to-all(s16[16,176,128]{2,1,0:T(8,128)(2,1)S(1)} %shard_map.123), channel_id=1, replica_groups={{0,32,64,96,128,160,192,224,256,288,320,352,384,416,448,480},{4,36,68,1..., dimensions={0} | all-to-all | bytes 1441792 | tf_op jit(solution)/shard_map/all_to_all | solution.py:391
  66.0 0.0 copy-done
  66.0 0.0 copy-done.1
  66.0 1.9 %shard_map.124 = (f32[9,49,256]{2,1,0:T(8,128)}, f32[9,256]{1,0:T(8,128)}, f32[49,256]{1,0:T(8,128)}, s32[1]{0:T(128)}) custom-call(s16[16,176,128]{2,1,0:T(8,128)(2,1)S(1)} %all_to_all.25.refs_0_, f32[9,49,256]{2,1,0:T(8,128)S(1)} %bitcast.5, f32[9,256]{1,0:T(8,128)S(1)} %copy-done.1), custom_call_target="tpu_custom_call" | custom-call | tf_op jit(solution)/shard_map/pallas_call | solution.py:401
  67.9 0.6 while.13
Async XLA Ops:
  1.8 19.6 %copy-start.2 = (s32[2,1024]{1,0:T(2,128)S(1)}, s32[2,1024]{1,0:T(2,128)}, u32[]{:S(2)}) copy-start(s32[2,1024]{1,0:T(2,128)} %cards.1) | copy-start | bytes 24580
  1.8 19.6 %copy-start.3 = (s32[4,256]{1,0:T(4,128)S(1)}, s32[4,256]{1,0:T(4,128)}, u32[]{:S(2)}) copy-start(s32[4,256]{1,0:T(4,128)} %ranks.1) | copy-start | bytes 12292
  1.9 19.5 %copy-start.4 = (s32[4,256]{1,0:T(4,128)S(1)}, s32[4,256]{1,0:T(4,128)}, u32[]{:S(2)}) copy-start(s32[4,256]{1,0:T(4,128)} %live.1) | copy-start | bytes 12292
  47.8 18.2 %copy-start = (f32[49,9,256]{2,0,1:T(8,128)S(1)}, f32[49,9,256]{2,0,1:T(8,128)}, u32[]{:S(2)}) copy-start(f32[49,9,256]{2,0,1:T(8,128)} %param.20) | copy-start | bytes 1354756
  47.8 18.2 %copy-start.1 = (f32[9,256]{1,0:T(8,128)S(1)}, f32[9,256]{1,0:T(8,128)}, u32[]{:S(2)}) copy-start(f32[9,256]{1,0:T(8,128)} %refs_2_.1) | copy-start | bytes 27652

commit v7 on v6

--- a/solution.py
+++ b/solution.py
@@ -256,6 +256,7 @@
     ]
     held = jnp.concatenate([tail[at + 3 : at + 4] for tail in tails], axis=0)
     cards[0] = jnp.max(held).astype(jnp.int32)
+    leasts = [jnp.max(tail[at + 2 : at + 3]).astype(jnp.int32) for tail in tails]
     dense[...] = jnp.zeros_like(dense)
     flops = jnp.zeros((32, 128), jnp.float32)
     for k in range(count):
@@ -263,7 +264,7 @@
         early = codes[:128] * scales[0][:, k : k + 1]
         late = codes[128:] * scales[1][:48, k : k + 1]
         flops += late[16:48]
-        least = jnp.max(tails[k][at + 2 : at + 3]).astype(jnp.int32)
+        least = leasts[k]
         for column in range(actions * halves):
             start = column * PAGE
             tile = early[start : start + PAGE] if start < 128 else late[start - 128 : start - 128 + PAGE]

time: 68.8 us -> 68.4 us (level)
  no operation moved by 1% of the time
where the time goes in v7:
time: 68.4 us; the launch traced here: 68.2 us
  blocking collectives  62.2 us (91%)
  Pallas kernels  4.66 us (7%)
  between operations  0.71 us (1%)
    all_to_all x2, blocking collectives, swap(): lax.all_to_all(blocks, 'turn', 0, 0, axis_index_groups=groups, tiled=True)  42.6 us
    all_gather x1, blocking collectives, shards(): gathered = lax.all_gather(payload, 'hand', axis=0, tiled=False)  19.5 us
    pallas_call x2, Pallas kernels, call(): pl.pallas_call(kernel, out_shape=jax.ShapeDtypeStruct(shape, jnp.int16),...  1.91 us
    pallas_call x1, Pallas kernels, shards(): pl.pallas_call(lambda *refs: finish(*factors, *refs), out_shape=outputs +...  1.56 us

profile of v7, /device:TPU:32, one launch (start us, length us, event | category | flops | bytes accessed | tf_op | source)
XLA Modules:
  0.0 68.2 jit_solution(16980886564427779318)
XLA Ops:
  0.6 1.2 %shard_map.121 = f32[2,80,128]{2,1,0:T(8,128)S(1)} custom-call(f32[81]{0:T(128)} %pot_hbm.1, s32[81]{0:T(128)} %turn_hbm.1, s32[81]{0:T(128)} %flop_hbm.1, s32[4]{0:T(128)} %of_hbm.1, bf16[81,4,256]{2,1,0:T(4,128)(2,1)} %bitcast.9, s32[4,256]{1,0:T(4,128)} %ranks.1, s32[4,256]{1,0:T(4,128)} %live.1), custom_call_target="tpu_custom_call" | custom-call | tf_op jit(solution)/shard_map/pallas_call | solution.py:349
  1.8 0.0 copy-start.2
  1.8 0.0 copy-start.3
  1.9 0.0 copy-start.4
  1.9 19.5 %all-gather = f32[8,80,128]{2,1,0:T(8,128)S(1)} all-gather(f32[2,80,128]{2,1,0:T(8,128)S(1)} %shard_map.121), channel_id=2, replica_groups=mesh['turn'=128,'hand'=4] {'hand'}, dimensions={0}, use_global_device_ids=true | all-gather | bytes 409600 | tf_op jit(solution)/shard_map/all_gather | solution.py:368
  21.4 0.0 copy-done.2
  21.4 0.0 copy-done.3
  21.4 0.0 copy-done.4
  21.4 1.2 %shard_map.122 = s16[8,96,128]{2,1,0:T(8,128)(2,1)S(1)} custom-call(f32[4,2,80,128]{3,2,1,0:T(8,128)S(1)} %bitcast.7, s32[4,256]{1,0:T(4,128)S(1)} %copy-done.3, s32[4,256]{1,0:T(4,128)S(1)} %copy-done.4, s32[2,1024]{1,0:T(2,128)S(1)} %copy-done.2), custom_call_target="tpu_custom_call" | custom-call | tf_op jit(solution)/shard_map/pallas_call | solution.py:382
  22.6 24.5 %all_to_all.24.blocks = s16[8,96,128]{2,1,0:T(8,128)(2,1)S(1)} all-to-all(s16[8,96,128]{2,1,0:T(8,128)(2,1)S(1)} %shard_map.122), channel_id=1, replica_groups={{0,4,8,12,16,20,24,28},{32,36,40,44,48,52,56,60},{64,68,72,76,80,84,88,..., dimensions={0} | all-to-all | bytes 393216 | tf_op jit(solution)/shard_map/all_to_all | solution.py:392
  47.1 0.7 shard_map.123
  47.8 0.0 copy-start
  47.8 0.0 copy-start.1
  47.8 18.2 %all_to_all.25.refs_0_ = s16[16,176,128]{2,1,0:T(8,128)(2,1)S(1)} all-to-all(s16[16,176,128]{2,1,0:T(8,128)(2,1)S(1)} %shard_map.123), channel_id=1, replica_groups={{0,32,64,96,128,160,192,224,256,288,320,352,384,416,448,480},{4,36,68,1..., dimensions={0} | all-to-all | bytes 1441792 | tf_op jit(solution)/shard_map/all_to_all | solution.py:392
  66.0 0.0 copy-done
  66.0 0.0 copy-done.1
  66.0 1.6 %shard_map.124 = (f32[9,49,256]{2,1,0:T(8,128)}, f32[9,256]{1,0:T(8,128)}, f32[49,256]{1,0:T(8,128)}, s32[1]{0:T(128)}) custom-call(s16[16,176,128]{2,1,0:T(8,128)(2,1)S(1)} %all_to_all.25.refs_0_, f32[9,49,256]{2,1,0:T(8,128)S(1)} %bitcast.5, f32[9,256]{1,0:T(8,128)S(1)} %copy-done.1), custom_call_target="tpu_custom_call" | custom-call | tf_op jit(solution)/shard_map/pallas_call | solution.py:402
  67.6 0.6 while.13
Async XLA Ops:
  1.8 19.6 %copy-start.2 = (s32[2,1024]{1,0:T(2,128)S(1)}, s32[2,1024]{1,0:T(2,128)}, u32[]{:S(2)}) copy-start(s32[2,1024]{1,0:T(2,128)} %cards.1) | copy-start | bytes 24580
  1.8 19.6 %copy-start.3 = (s32[4,256]{1,0:T(4,128)S(1)}, s32[4,256]{1,0:T(4,128)}, u32[]{:S(2)}) copy-start(s32[4,256]{1,0:T(4,128)} %ranks.1) | copy-start | bytes 12292
  1.9 19.5 %copy-start.4 = (s32[4,256]{1,0:T(4,128)S(1)}, s32[4,256]{1,0:T(4,128)}, u32[]{:S(2)}) copy-start(s32[4,256]{1,0:T(4,128)} %live.1) | copy-start | bytes 12292
  47.8 18.2 %copy-start = (f32[49,9,256]{2,0,1:T(8,128)S(1)}, f32[49,9,256]{2,0,1:T(8,128)}, u32[]{:S(2)}) copy-start(f32[49,9,256]{2,0,1:T(8,128)} %param.20) | copy-start | bytes 1354756
  47.8 18.2 %copy-start.1 = (f32[9,256]{1,0:T(8,128)S(1)}, f32[9,256]{1,0:T(8,128)}, u32[]{:S(2)}) copy-start(f32[9,256]{1,0:T(8,128)} %refs_2_.1) | copy-start | bytes 27652

commit v8 on v7

--- a/solution.py
+++ b/solution.py
@@ -60,13 +60,20 @@
         yield codes * scales[:64, k : k + 1]
 
 
+def row_tops(pot, turn_act, flop_act, count):
+    row = lax.broadcasted_iota(jnp.int32, (24, pot.shape[1]), 0)
+    key = jnp.where(row < count, turn_act[...], flop_act[...] + count)
+    return jnp.sum(jnp.where(row == key, pot[...], 0.0), axis=1, keepdims=True)
+
+
 def weigh(
-    pot_hbm, turn_hbm, flop_hbm, of_hbm, reach_hbm, ranks_hbm, live_hbm, out,
-    pot, turn_act, flop_act, turn_of, reach, ranks, live, sems, *banks
+    pot_hbm, turn_hbm, flop_hbm, of_hbm, reach_hbm, ranks_hbm, live_hbm, pots_hbm, turns_hbm, flops_hbm, out,
+    pot, turn_act, flop_act, turn_of, reach, ranks, live, pots, turns, flops, stage, sems, *banks
 ):
     pairs = (
         (reach_hbm, reach), (pot_hbm, pot), (turn_hbm, turn_act), (flop_hbm, flop_act),
         (of_hbm, turn_of), (ranks_hbm, ranks), (live_hbm, live),
+        (pots_hbm, pots), (turns_hbm, turns), (flops_hbm, flops),
     )
     moves = [pltpu.make_async_copy(x, y, sems.at[k]) for k, (x, y) in enumerate(pairs)]
     for move in moves:
@@ -83,24 +90,28 @@
         turn_sums[s % BANKS][turn_act[s]] += term
         flop_sums[s % BANKS][flop_act[s]] += term
     alive = live[...].astype(jnp.float32)
+    steps = 65535.0 / jnp.maximum(row_tops(pots, turns, flops, turn_sums[0].shape[0]), 1e-30)
     top = 0
     for sums in (turn_sums, flop_sums):
         for r in range(sums[0].shape[0]):
             total = sums[0][r]
             for other in sums[1:]:
                 total += other[r]
-            total *= alive
+            at = top // boards
+            total = jnp.round(total * alive * steps[at : at + 1])
+            total = jnp.minimum(total, 65535.0) - 32768.0
             for half, lanes in enumerate(halves):
-                out[half, pl.ds(top, boards), :] = total[:, lanes]
+                stage[half, pl.ds(top, boards), :] = total[:, lanes]
             top += boards
     for half, lanes in enumerate(halves):
-        out[half, pl.ds(top, boards), :] = ranks[:, lanes].astype(jnp.float32)
+        stage[half, pl.ds(top, boards), :] = ranks[:, lanes].astype(jnp.float32)
         for b in range(boards):
             card = jnp.full((1, 128), turn_of[b], jnp.int32).astype(jnp.float32)
-            out[half, pl.ds(top + boards + b, 1), :] = card
-
-
-def board_values(payload, ranks, live, cards):
+            stage[half, pl.ds(top + boards + b, 1), :] = card
+    out[...] = stage[...].astype(jnp.int32).astype(jnp.int16)
+
+
+def board_values(payload, ranks, live, cards, pot, turn_act, flop_act, wide):
     hands, halves, rows, _ = payload.shape
     width = halves * 128
     boards = ranks.shape[0]
@@ -120,30 +131,34 @@
         aparts.append(jnp.where(shared, 0.0, 1.0))
     apart = jnp.concatenate(aparts, axis=1)
     tall = -(-each // 8) * 8
+    wide[...] = payload[...].astype(jnp.int32).astype(jnp.float32)
+    unit = row_tops(pot, turn_act, flop_act, (each - 2) // 2) * (1.0 / 65535.0)
     sums, turn_cards = [], []
     for b in range(boards):
         x = jnp.concatenate(
-            [payload[h, half, pl.ds(b, each, stride=boards), :] for h in range(hands) for half in range(halves)],
+            [wide[h, half, pl.ds(b, each, stride=boards), :] for h in range(hands) for half in range(halves)],
             axis=1,
         )
         theirs = x[each - 2 : each - 1]
         turn_cards.append(x[each - 1 : each, :128])
         x = jnp.concatenate([x, jnp.zeros((tall - each, hands * width), jnp.float32)], axis=0)
-        high = x.astype(jnp.bfloat16).astype(jnp.float32)
-        mid = (x - high).astype(jnp.bfloat16).astype(jnp.float32)
-        pieces = jnp.concatenate([high, mid, x - high - mid], axis=0).astype(jnp.bfloat16)
+        x += 32768.0
+        high = jnp.floor(x * (1.0 / 256.0))
+        pieces = jnp.concatenate([high, x - high * 256.0], axis=0).astype(jnp.bfloat16)
         sign = jnp.clip(columns[:, b : b + 1] - theirs, -1.0, 1.0)
         tile = (sign * apart).astype(jnp.bfloat16)
         part = lax.dot_general(
             pieces, tile, (((1,), (1,)), ((), ())), preferred_element_type=jnp.float32
         )
-        part = part[:tall] + (part[tall : 2 * tall] + part[2 * tall :])
+        part = (part[:tall] * 256.0 + part[tall:]) * unit
         sums.append(part * live[b : b + 1, :].astype(jnp.float32))
     return sums, turn_cards, (each - 2) // 2
 
 
-def showdown_all(payload, ranks, live, cards, out, dense):
-    sums, turn_cards, actions = board_values(payload, ranks, live, cards)
+def showdown_all(payload, ranks, live, cards, pot, turn_act, flop_act, out, dense, wide):
+    sums, turn_cards, actions = board_values(
+        payload, ranks, live, cards, pot, turn_act, flop_act, wide
+    )
     width = sums[0].shape[1]
     flops = sums[0]
     for part in sums[1:]:
@@ -167,8 +182,10 @@
         out[k] = pack(dense[pl.ds(k * CHUNK, CHUNK), :])
 
 
-def showdown(payload, ranks, live, cards, out, rows):
-    sums, turn_cards, actions = board_values(payload, ranks, live, cards)
+def showdown(payload, ranks, live, cards, pot, turn_act, flop_act, out, rows, wide):
+    sums, turn_cards, actions = board_values(
+        payload, ranks, live, cards, pot, turn_act, flop_act, wide
+    )
     halves = sums[0].shape[1] // 128
     flops = sums[0]
     for part in sums[1:]:
@@ -345,11 +362,12 @@
     params = pltpu.CompilerParams(vmem_limit_bytes=VMEM)
     f32 = jnp.float32
 
-    operands = (pot, turn_act, flop_act, turn_of, jnp.transpose(reach, (1, 0, 2)), ranks, live)
+    acts = tuple(x.reshape(1, seqs) for x in (pot, turn_act, flop_act))
+    operands = (pot, turn_act, flop_act, turn_of, jnp.transpose(reach, (1, 0, 2)), ranks, live) + acts
     payload = pl.pallas_call(
         weigh,
-        out_shape=jax.ShapeDtypeStruct((width // 128, rows + 2 * boards, 128), f32),
-        in_specs=[pl.BlockSpec(memory_space=pltpu.HBM)] * 7,
+        out_shape=jax.ShapeDtypeStruct((width // 128, rows + 2 * boards, 128), jnp.int16),
+        in_specs=[pl.BlockSpec(memory_space=pltpu.HBM)] * 10,
         out_specs=pl.BlockSpec(memory_space=pltpu.VMEM),
         scratch_shapes=[
             pltpu.SMEM(pot.shape, f32),
@@ -359,7 +377,9 @@
             pltpu.VMEM((seqs, boards, width), reach.dtype),
             pltpu.VMEM(ranks.shape, jnp.int32),
             pltpu.VMEM(live.shape, jnp.int32),
-            pltpu.SemaphoreType.DMA((7,)),
+            *[pltpu.VMEM((1, seqs), x.dtype) for x in acts],
+            pltpu.VMEM((width // 128, rows + 2 * boards, 128), f32),
+            pltpu.SemaphoreType.DMA((10,)),
             *[pltpu.VMEM((actions, boards, width), f32)] * (2 * BANKS),
         ],
         compiler_params=params,
@@ -392,7 +412,8 @@
         return lax.all_to_all(blocks, "turn", 0, 0, axis_index_groups=groups, tiled=True)
 
     blocks = call(
-        showdown, (LINE, BOARD_ROWS, 128), [(BOARD_ROWS, 128)], gathered, ranks, live, hand_cards
+        showdown, (LINE, BOARD_ROWS, 128), [(BOARD_ROWS, 128), gathered.shape],
+        gathered, ranks, live, hand_cards, *acts
     )
     blocks = swap(blocks, lines)
     blocks = call(
@@ -409,10 +430,10 @@
     )(blocks, by_action, flop_regret)
 
     def every_card(state):
-        payload = gathered + jnp.where(state[0] > PAGE, 0.0, 1.0)
-        scratch = [(UNITS * 8, 128)]
+        payload = gathered + jnp.where(state[0] > PAGE, 0, 1).astype(jnp.int16)
+        scratch = [(UNITS * 8, 128), gathered.shape]
         chunks = call(
-            showdown_all, (PLANE, CHUNK, 128), scratch, payload, ranks, live, hand_cards
+            showdown_all, (PLANE, CHUNK, 128), scratch, payload, ranks, live, hand_cards, *acts
         )
         chunks = swap(chunks, planes)
         chunks = swap(call(add_up, (LINE, CHUNK, 128), [], chunks), lines)

time: 68.4 us -> 113 us (1.65)
  the two profiles are of different devices: /device:TPU:32 before, /device:TPU:2 now
where the time goes in v8:
time: 113 us
  blocking collectives  100 us (88%)
  Pallas kernels  8.42 us (7%)
  loops' own time  2.49 us (2%)
    all_to_all x5, blocking collectives, swap(): lax.all_to_all(blocks, 'turn', 0, 0, axis_index_groups=groups, tiled=True)  82.7 us
    all_gather x1, blocking collectives, shards(): gathered = lax.all_gather(payload, 'hand', axis=0, tiled=False)  17.7 us
    pallas_call x5, Pallas kernels, call(): pl.pallas_call(kernel, out_shape=jax.ShapeDtypeStruct(shape, jnp.int16),...  4.4 us
    another operation x1, loops' own time, shards(): lax.while_loop(lambda s: s[0] > PAGE, every_card, state)  2.49 us

profile of v8, /device:TPU:2, one launch (start us, length us, event | category | flops | bytes accessed | tf_op | source)
XLA Modules:
  0.0 112.8 jit_solution(5310007724156311089)
XLA Ops:
  0.6 1.3 %shard_map.121 = s16[2,80,128]{2,1,0:T(8,128)(2,1)S(1)} custom-call(f32[81]{0:T(128)} %pot_hbm.1, s32[81]{0:T(128)} %turn_hbm.1, s32[81]{0:T(128)} %flop_hbm.1, s32[4]{0:T(128)} %of_hbm.1, bf16[81,4,256]{2,1,0:T(4,128)(2,1)} %bitcast.12, s32[4,256]{1,0:T(4,128)} %ranks.1, s32[4,256]{1,0:T(4,128)} %live.1, f32[1,81]{1,0:T(1,128)} %bitcast.13, ...), custom_call_target="tpu_custom_call" | custom-call | tf_op jit(solution)/shard_map/pallas_call | solution.py:367
  1.9 0.0 copy-start.2
  1.9 0.0 copy-start.3
  1.9 0.0 copy-start.4
  1.9 17.7 %all-gather = s16[8,80,128]{2,1,0:T(8,128)(2,1)S(1)} all-gather(s16[2,80,128]{2,1,0:T(8,128)(2,1)S(1)} %shard_map.121), channel_id=2, replica_groups=mesh['turn'=128,'hand'=4] {'hand'}, dimensions={0}, use_global_device_ids=true | all-gather | bytes 204800 | tf_op jit(solution)/shard_map/all_gather | solution.py:388
  19.7 0.0 copy-start.5
  19.7 0.0 copy-start.6
  19.7 0.0 copy-start.7
  19.7 0.0 copy-done.2
  19.7 0.0 copy-done.3
  19.7 0.0 copy-done.4
  19.7 0.6 copy-done.5
  20.3 0.0 copy-done.6
  20.3 0.0 copy-done.7
  20.3 1.3 %shard_map.122 = s16[8,96,128]{2,1,0:T(8,128)(2,1)S(1)} custom-call(s16[4,2,80,128]{3,2,1,0:T(8,128)(2,1)S(1)} %bitcast.10, s32[4,256]{1,0:T(4,128)S(1)} %copy-done.3, s32[4,256]{1,0:T(4,128)S(1)} %copy-done.4, s32[2,1024]{1,0:T(2,128)S(1)} %copy-done.2, f32[1,81]{1,0:T(1,128)S(1)} %bitcast.14, s32[1,81]{1,0:T(1,128)S(1)} %bitcast.17, s32[1,81]{1,0:T(1,128)S(1)} %bitcast.20), custom_call_target="tpu_custom_call" | custom-call | tf_op jit(solution)/shard_map/pallas_call | solution.py:402
  21.6 23.4 %all_to_all.25.blocks = s16[8,96,128]{2,1,0:T(8,128)(2,1)S(1)} all-to-all(s16[8,96,128]{2,1,0:T(8,128)(2,1)S(1)} %shard_map.122), channel_id=1, replica_groups={{0,4,8,12,16,20,24,28},{32,36,40,44,48,52,56,60},{64,68,72,76,80,84,88,..., dimensions={0} | all-to-all | bytes 393216 | tf_op jit(solution)/shard_map/all_to_all | solution.py:412
  45.1 0.7 shard_map.123
  45.8 0.0 copy-start
  45.8 0.0 copy-start.1
  45.8 17.2 %all_to_all.26.refs_0_ = s16[16,176,128]{2,1,0:T(8,128)(2,1)S(1)} all-to-all(s16[16,176,128]{2,1,0:T(8,128)(2,1)S(1)} %shard_map.123), channel_id=1, replica_groups={{0,32,64,96,128,160,192,224,256,288,320,352,384,416,448,480},{4,36,68,1..., dimensions={0} | all-to-all | bytes 1441792 | tf_op jit(solution)/shard_map/all_to_all | solution.py:412
  63.0 0.0 copy-done
  63.0 0.0 copy-done.1
  63.0 1.6 %shard_map.124 = (f32[9,49,256]{2,1,0:T(8,128)}, f32[9,256]{1,0:T(8,128)}, f32[49,256]{1,0:T(8,128)}, s32[1]{0:T(128)}) custom-call(s16[16,176,128]{2,1,0:T(8,128)(2,1)S(1)} %all_to_all.26.refs_0_, f32[9,49,256]{2,1,0:T(8,128)S(1)} %bitcast.8, f32[9,256]{1,0:T(8,128)S(1)} %copy-done.1), custom_call_target="tpu_custom_call" | custom-call | tf_op jit(solution)/shard_map/pallas_call | solution.py:423
  64.6 48.3 %while.13 = (s32[]{:T(128)}, f32[9,49,256]{2,1,0:T(8,128)}, f32[9,256]{1,0:T(8,128)}, f32[49,256]{1,0:T(8,128)}, s16[4,2,80,128]{3,2,1,0:T(8,128)(2,1)S(1)}, /*i...) while((s32[]{:T(128)}, f32[9,49,256]{2,1,0:T(8,128)}, ...), condition=%region_1.2_spmd, body=%region_0.1_spmd | while | flops 81924 | bytes 1638559 | solution.py:452
  65.9 1.6 %body.4 = s16[16,64,128]{2,1,0:T(8,128)(2,1)S(1)} custom-call(s16[4,2,80,128]{3,2,1,0:T(8,128)(2,1)S(1)} %broadcast_add_fusion.payload, s32[4,256]{1,0:T(4,128)S(1)} %get-tuple-element.153.ranks, s32[4,256]{1,0:T(4,128)S(1)} %get-tuple-element.154.live, s32[2,1024]{1,0:T(2,128)S(1)} %get-tuple-element.155.cards, f32[1,81]{1,0:T(1,128)S(1)} %get-tuple-element.156.pot, ...), custom_call_target="tpu_custom_call" | custom-call | tf_op jit(solution)/shard_map/while/body/pallas_call | solution.py:402
  67.4 11.7 %all_to_all.22.blocks = s16[16,64,128]{2,1,0:T(8,128)(2,1)S(1)} all-to-all(s16[16,64,128]{2,1,0:T(8,128)(2,1)S(1)} %body.4), channel_id=1, replica_groups={{0,32,64,96,128,160,192,224,256,288,320,352,384,416,448,480},{4,36,68,1..., dimensions={0} | all-to-all | bytes 524288 | tf_op jit(solution)/shard_map/while/body/all_to_all | solution.py:412
  79.1 0.5 body.5
  79.6 18.9 %all_to_all.23.blocks = s16[8,64,128]{2,1,0:T(8,128)(2,1)S(1)} all-to-all(s16[8,64,128]{2,1,0:T(8,128)(2,1)S(1)} %body.5), channel_id=1, replica_groups={{0,4,8,12,16,20,24,28},{32,36,40,44,48,52,56,60},{64,68,72,76,80,84,88,..., dimensions={0} | all-to-all | bytes 262144 | tf_op jit(solution)/shard_map/while/body/all_to_all | solution.py:412
  98.4 0.4 body.6
  98.8 11.6 %all_to_all.24.refs_0_ = s16[16,64,128]{2,1,0:T(8,128)(2,1)S(1)} all-to-all(s16[16,64,128]{2,1,0:T(8,128)(2,1)S(1)} %body.6), channel_id=1, replica_groups={{0,32,64,96,128,160,192,224,256,288,320,352,384,416,448,480},{4,36,68,1..., dimensions={0} | all-to-all | bytes 524288 | tf_op jit(solution)/shard_map/while/body/all_to_all | solution.py:412
  110.4 1.2 %body.7 = (f32[9,49,256]{2,1,0:T(8,128)}, f32[9,256]{1,0:T(8,128)}, f32[49,256]{1,0:T(8,128)}) custom-call(s16[16,64,128]{2,1,0:T(8,128)(2,1)S(1)} %all_to_all.24.refs_0_, f32[9,49,256]{2,1,0:T(8,128)S(1)} %get-tuple-element.159.refs_1_, f32[9,256]{1,0:T(8,128)S(1)} %get-tuple-element.160.refs_2_), custom_call_target="tpu_custom_call" | custom-call | tf_op jit(solution)/shard_map/while/body/pallas_call | solution.py:441
  (1 shorter events, 0.0 us)
Async XLA Ops:
  1.9 17.8 %copy-start.2 = (s32[2,1024]{1,0:T(2,128)S(1)}, s32[2,1024]{1,0:T(2,128)}, u32[]{:S(2)}) copy-start(s32[2,1024]{1,0:T(2,128)} %cards.1) | copy-start | bytes 24580
  1.9 17.8 %copy-start.3 = (s32[4,256]{1,0:T(4,128)S(1)}, s32[4,256]{1,0:T(4,128)}, u32[]{:S(2)}) copy-start(s32[4,256]{1,0:T(4,128)} %ranks.1) | copy-start | bytes 12292
  1.9 17.8 %copy-start.4 = (s32[4,256]{1,0:T(4,128)S(1)}, s32[4,256]{1,0:T(4,128)}, u32[]{:S(2)}) copy-start(s32[4,256]{1,0:T(4,128)} %live.1) | copy-start | bytes 12292
  19.7 0.7 copy-start.5
  19.7 0.7 copy-start.6
  19.7 0.7 copy-start.7
  45.8 17.2 %copy-start = (f32[49,9,256]{2,0,1:T(8,128)S(1)}, f32[49,9,256]{2,0,1:T(8,128)}, u32[]{:S(2)}) copy-start(f32[49,9,256]{2,0,1:T(8,128)} %param.20) | copy-start | bytes 1354756
  45.8 17.2 %copy-start.1 = (f32[9,256]{1,0:T(8,128)S(1)}, f32[9,256]{1,0:T(8,128)}, u32[]{:S(2)}) copy-start(f32[9,256]{1,0:T(8,128)} %refs_2_.1) | copy-start | bytes 27652

commit v9 on v8

--- a/solution.py
+++ b/solution.py
@@ -67,7 +67,7 @@
 
 
 def weigh(
-    pot_hbm, turn_hbm, flop_hbm, of_hbm, reach_hbm, ranks_hbm, live_hbm, pots_hbm, turns_hbm, flops_hbm, out,
+    pot_hbm, turn_hbm, flop_hbm, of_hbm, reach_hbm, ranks_hbm, live_hbm, pots_hbm, turns_hbm, flops_hbm, out, tops,
     pot, turn_act, flop_act, turn_of, reach, ranks, live, pots, turns, flops, stage, sems, *banks
 ):
     pairs = (
@@ -90,7 +90,9 @@
         turn_sums[s % BANKS][turn_act[s]] += term
         flop_sums[s % BANKS][flop_act[s]] += term
     alive = live[...].astype(jnp.float32)
-    steps = 65535.0 / jnp.maximum(row_tops(pots, turns, flops, turn_sums[0].shape[0]), 1e-30)
+    most = row_tops(pots, turns, flops, turn_sums[0].shape[0])
+    tops[...] = jnp.broadcast_to(most, tops.shape)
+    steps = 65535.0 / jnp.maximum(most, 1e-30)
     top = 0
     for sums in (turn_sums, flop_sums):
         for r in range(sums[0].shape[0]):
@@ -111,7 +113,7 @@
     out[...] = stage[...].astype(jnp.int32).astype(jnp.int16)
 
 
-def board_values(payload, ranks, live, cards, pot, turn_act, flop_act, wide):
+def board_values(payload, tops, ranks, live, cards, wide):
     hands, halves, rows, _ = payload.shape
     width = halves * 128
     boards = ranks.shape[0]
@@ -132,7 +134,7 @@
     apart = jnp.concatenate(aparts, axis=1)
     tall = -(-each // 8) * 8
     wide[...] = payload[...].astype(jnp.int32).astype(jnp.float32)
-    unit = row_tops(pot, turn_act, flop_act, (each - 2) // 2) * (1.0 / 65535.0)
+    unit = tops[:, 0:1] * (1.0 / 65535.0)
     sums, turn_cards = [], []
     for b in range(boards):
         x = jnp.concatenate(
@@ -155,10 +157,8 @@
     return sums, turn_cards, (each - 2) // 2
 
 
-def showdown_all(payload, ranks, live, cards, pot, turn_act, flop_act, out, dense, wide):
-    sums, turn_cards, actions = board_values(
-        payload, ranks, live, cards, pot, turn_act, flop_act, wide
-    )
+def showdown_all(payload, tops, ranks, live, cards, out, dense, wide):
+    sums, turn_cards, actions = board_values(payload, tops, ranks, live, cards, wide)
     width = sums[0].shape[1]
     flops = sums[0]
     for part in sums[1:]:
@@ -182,10 +182,8 @@
         out[k] = pack(dense[pl.ds(k * CHUNK, CHUNK), :])
 
 
-def showdown(payload, ranks, live, cards, pot, turn_act, flop_act, out, rows, wide):
-    sums, turn_cards, actions = board_values(
-        payload, ranks, live, cards, pot, turn_act, flop_act, wide
-    )
+def showdown(payload, tops, ranks, live, cards, out, rows, wide):
+    sums, turn_cards, actions = board_values(payload, tops, ranks, live, cards, wide)
     halves = sums[0].shape[1] // 128
     flops = sums[0]
     for part in sums[1:]:
@@ -364,11 +362,14 @@
 
     acts = tuple(x.reshape(1, seqs) for x in (pot, turn_act, flop_act))
     operands = (pot, turn_act, flop_act, turn_of, jnp.transpose(reach, (1, 0, 2)), ranks, live) + acts
-    payload = pl.pallas_call(
+    payload, tops = pl.pallas_call(
         weigh,
-        out_shape=jax.ShapeDtypeStruct((width // 128, rows + 2 * boards, 128), jnp.int16),
+        out_shape=(
+            jax.ShapeDtypeStruct((width // 128, rows + 2 * boards, 128), jnp.int16),
+            jax.ShapeDtypeStruct((24, 128), f32),
+        ),
         in_specs=[pl.BlockSpec(memory_space=pltpu.HBM)] * 10,
-        out_specs=pl.BlockSpec(memory_space=pltpu.VMEM),
+        out_specs=tuple(spread(2)),
         scratch_shapes=[
             pltpu.SMEM(pot.shape, f32),
             pltpu.SMEM(turn_act.shape, jnp.int32),
@@ -413,7 +414,7 @@
 
     blocks = call(
         showdown, (LINE, BOARD_ROWS, 128), [(BOARD_ROWS, 128), gathered.shape],
-        gathered, ranks, live, hand_cards, *acts
+        gathered, tops, ranks, live, hand_cards
     )
     blocks = swap(blocks, lines)
     blocks = call(
@@ -433,7 +434,7 @@
         payload = gathered + jnp.where(state[0] > PAGE, 0, 1).astype(jnp.int16)
         scratch = [(UNITS * 8, 128), gathered.shape]
         chunks = call(
-            showdown_all, (PLANE, CHUNK, 128), scratch, payload, ranks, live, hand_cards, *acts
+            showdown_all, (PLANE, CHUNK, 128), scratch, payload, tops, ranks, live, hand_cards
         )
         chunks = swap(chunks, planes)
         chunks = swap(call(add_up, (LINE, CHUNK, 128), [], chunks), lines)

time: 113 us -> 65.6 us (0.58)
  the two profiles are of different devices: /device:TPU:2 before, /device:TPU:32 now
where the time goes in v9:
time: 65.6 us; the launch traced here: 65.3 us
  blocking collectives  59.2 us (90%)
  Pallas kernels  4.78 us (7%)
  between operations  0.71 us (1%)
    all_to_all x2, blocking collectives, swap(): lax.all_to_all(blocks, 'turn', 0, 0, axis_index_groups=groups, tiled=True)  42.5 us
    all_gather x1, blocking collectives, shards(): gathered = lax.all_gather(payload, 'hand', axis=0, tiled=False)  16.7 us
    pallas_call x2, Pallas kernels, call(): pl.pallas_call(kernel, out_shape=jax.ShapeDtypeStruct(shape, jnp.int16),...  1.97 us
    pallas_call x1, Pallas kernels, shards(): pl.pallas_call(lambda *refs: finish(*factors, *refs), out_shape=outputs +...  1.56 us

profile of v9, /device:TPU:32, one launch (start us, length us, event | category | flops | bytes accessed | tf_op | source)
XLA Modules:
  0.0 65.3 jit_solution(11359816710635866107)
XLA Ops:
  0.6 1.2 %shard_map.121 = (s16[2,80,128]{2,1,0:T(8,128)(2,1)S(1)}, f32[24,128]{1,0:T(8,128)S(1)}) custom-call(f32[81]{0:T(128)} %pot_hbm.1, s32[81]{0:T(128)} %turn_hbm.1, s32[81]{0:T(128)} %flop_hbm.1, s32[4]{0:T(128)} %of_hbm.1, bf16[81,4,256]{2,1,0:T(4,128)(2,1)} %bitcast.12, s32[4,256]{1,0:T(4,128)} %ranks.1, s32[4,256]{1,0:T(4,128)} %live.1, f32[1,81]{1,0:T(1,128)} %bitcast.13, ...), custom_call_target="tpu_custom_call" | custom-call | tf_op jit(solution)/shard_map/pallas_call | solution.py:365
  1.9 0.0 copy-start.2
  1.9 0.0 copy-start.3
  1.9 0.0 copy-start.4
  1.9 16.7 %all-gather = s16[8,80,128]{2,1,0:T(8,128)(2,1)S(1)} all-gather(s16[2,80,128]{2,1,0:T(8,128)(2,1)S(1)} %get-tuple-element.68), channel_id=2, replica_groups=mesh['turn'=128,'hand'=4] {'hand'}, dimensions={0}, use_global_device_ids=true | all-gather | bytes 204800 | tf_op jit(solution)/shard_map/all_gather | solution.py:389
  18.6 0.0 copy-done.2
  18.6 0.0 copy-done.3
  18.6 0.0 copy-done.4
  18.6 1.3 %shard_map.122 = s16[8,96,128]{2,1,0:T(8,128)(2,1)S(1)} custom-call(s16[4,2,80,128]{3,2,1,0:T(8,128)(2,1)S(1)} %bitcast.10, f32[24,128]{1,0:T(8,128)S(1)} %get-tuple-element.115.tops, s32[4,256]{1,0:T(4,128)S(1)} %copy-done.3, s32[4,256]{1,0:T(4,128)S(1)} %copy-done.4, s32[2,1024]{1,0:T(2,128)S(1)} %copy-done.2), custom_call_target="tpu_custom_call" | custom-call | tf_op jit(solution)/shard_map/pallas_call | solution.py:403
  19.9 24.1 %all_to_all.25.blocks = s16[8,96,128]{2,1,0:T(8,128)(2,1)S(1)} all-to-all(s16[8,96,128]{2,1,0:T(8,128)(2,1)S(1)} %shard_map.122), channel_id=1, replica_groups={{0,4,8,12,16,20,24,28},{32,36,40,44,48,52,56,60},{64,68,72,76,80,84,88,..., dimensions={0} | all-to-all | bytes 393216 | tf_op jit(solution)/shard_map/all_to_all | solution.py:413
  44.0 0.7 %shard_map.123 = s16[16,176,128]{2,1,0:T(8,128)(2,1)S(1)} custom-call(s16[8,96,128]{2,1,0:T(8,128)(2,1)S(1)} %all_to_all.25.blocks), custom_call_target="tpu_custom_call" | custom-call | tf_op jit(solution)/shard_map/pallas_call | solution.py:403
  44.7 0.0 copy-start
  44.7 0.0 copy-start.1
  44.7 18.4 %all_to_all.26.refs_0_ = s16[16,176,128]{2,1,0:T(8,128)(2,1)S(1)} all-to-all(s16[16,176,128]{2,1,0:T(8,128)(2,1)S(1)} %shard_map.123), channel_id=1, replica_groups={{0,32,64,96,128,160,192,224,256,288,320,352,384,416,448,480},{4,36,68,1..., dimensions={0} | all-to-all | bytes 1441792 | tf_op jit(solution)/shard_map/all_to_all | solution.py:413
  63.1 0.0 copy-done
  63.1 0.0 copy-done.1
  63.1 1.6 %shard_map.124 = (f32[9,49,256]{2,1,0:T(8,128)}, f32[9,256]{1,0:T(8,128)}, f32[49,256]{1,0:T(8,128)}, s32[1]{0:T(128)}) custom-call(s16[16,176,128]{2,1,0:T(8,128)(2,1)S(1)} %all_to_all.26.refs_0_, f32[9,49,256]{2,1,0:T(8,128)S(1)} %bitcast.8, f32[9,256]{1,0:T(8,128)S(1)} %copy-done.1), custom_call_target="tpu_custom_call" | custom-call | tf_op jit(solution)/shard_map/pallas_call | solution.py:424
  64.7 0.6 while.13
Async XLA Ops:
  1.9 16.7 %copy-start.2 = (s32[2,1024]{1,0:T(2,128)S(1)}, s32[2,1024]{1,0:T(2,128)}, u32[]{:S(2)}) copy-start(s32[2,1024]{1,0:T(2,128)} %cards.1) | copy-start | bytes 24580
  1.9 16.7 %copy-start.3 = (s32[4,256]{1,0:T(4,128)S(1)}, s32[4,256]{1,0:T(4,128)}, u32[]{:S(2)}) copy-start(s32[4,256]{1,0:T(4,128)} %ranks.1) | copy-start | bytes 12292
  1.9 16.7 %copy-start.4 = (s32[4,256]{1,0:T(4,128)S(1)}, s32[4,256]{1,0:T(4,128)}, u32[]{:S(2)}) copy-start(s32[4,256]{1,0:T(4,128)} %live.1) | copy-start | bytes 12292
  44.7 18.4 %copy-start = (f32[49,9,256]{2,0,1:T(8,128)S(1)}, f32[49,9,256]{2,0,1:T(8,128)}, u32[]{:S(2)}) copy-start(f32[49,9,256]{2,0,1:T(8,128)} %param.20) | copy-start | bytes 1354756
  44.7 18.4 %copy-start.1 = (f32[9,256]{1,0:T(8,128)S(1)}, f32[9,256]{1,0:T(8,128)}, u32[]{:S(2)}) copy-start(f32[9,256]{1,0:T(8,128)} %refs_2_.1) | copy-start | bytes 27652

commit v10 on v9

--- a/solution.py
+++ b/solution.py
@@ -212,7 +212,7 @@
         out[k] = codes
 
 
-def run_sums(blocks, out, rows, page):
+def run_sums(past, blocks, out, rows, page):
     count = blocks.shape[0]
     boards, halves, actions = 4, 2, 9
     tails = [blocks[k, 80:96, :].astype(jnp.int32).astype(jnp.float32) for k in range(count)]
@@ -227,7 +227,7 @@
     most = ids[-1][:, boards - 1 : boards]
     slot = lax.broadcasted_iota(jnp.int32, (PAGE, 128), 0).astype(jnp.float32)
     hits = [
-        [(slot == ids[k][:, b : b + 1] - least).astype(jnp.float32) for b in range(boards)]
+        [(slot + past == ids[k][:, b : b + 1] - least).astype(jnp.float32) for b in range(boards)]
         for k in range(count)
     ]
     page[...] = jnp.zeros_like(page)
@@ -257,33 +257,36 @@
         out[k] = codes
 
 
-def finish(turns_over_boards, over_boards, blocks, turn_regret, flop_regret, turn_out, flop_out, values, cards, dense):
+def finish(turns_over_boards, over_boards, pages, *refs):
+    turn_regret, flop_regret, turn_out, flop_out, values, cards, dense = refs[pages:]
     actions, turns, width = turn_regret.shape
-    halves, count = width // 128, blocks.shape[0]
+    halves, count = width // 128, refs[0].shape[0]
     at = PAGE_SCALES - 160
-    tails = [blocks[k, 160:176, :].astype(jnp.int32).astype(jnp.float32) for k in range(count)]
-    scales = [
-        jnp.transpose(
-            jnp.exp2(jnp.concatenate([tail[at + part : at + part + 1] for tail in tails], axis=0) * (1.0 / 256.0))
-            * (1.0 / STEPS)
-        )
-        for part in range(2)
-    ]
-    held = jnp.concatenate([tail[at + 3 : at + 4] for tail in tails], axis=0)
-    cards[0] = jnp.max(held).astype(jnp.int32)
-    leasts = [jnp.max(tail[at + 2 : at + 3]).astype(jnp.int32) for tail in tails]
     dense[...] = jnp.zeros_like(dense)
     flops = jnp.zeros((32, 128), jnp.float32)
-    for k in range(count):
-        codes = blocks[k].astype(jnp.int32).astype(jnp.float32)
-        early = codes[:128] * scales[0][:, k : k + 1]
-        late = codes[128:] * scales[1][:48, k : k + 1]
-        flops += late[16:48]
-        least = leasts[k]
-        for column in range(actions * halves):
-            start = column * PAGE
-            tile = early[start : start + PAGE] if start < 128 else late[start - 128 : start - 128 + PAGE]
-            dense[pl.ds(column * SPAN + least, PAGE), :] += tile
+    for page, blocks in enumerate(refs[:pages]):
+        tails = [blocks[k, 160:176, :].astype(jnp.int32).astype(jnp.float32) for k in range(count)]
+        scales = [
+            jnp.transpose(
+                jnp.exp2(jnp.concatenate([tail[at + part : at + part + 1] for tail in tails], axis=0) * (1.0 / 256.0))
+                * (1.0 / STEPS)
+            )
+            for part in range(2)
+        ]
+        if page == 0:
+            held = jnp.concatenate([tail[at + 3 : at + 4] for tail in tails], axis=0)
+            cards[0] = jnp.max(held).astype(jnp.int32)
+        leasts = [jnp.max(tail[at + 2 : at + 3]).astype(jnp.int32) for tail in tails]
+        for k in range(count):
+            codes = blocks[k].astype(jnp.int32).astype(jnp.float32)
+            early = codes[:128] * scales[0][:, k : k + 1]
+            late = codes[128:] * scales[1][:48, k : k + 1]
+            if page == 0:
+                flops += late[16:48]
+            for column in range(actions * halves):
+                start = column * PAGE
+                tile = early[start : start + PAGE] if start < 128 else late[start - 128 : start - 128 + PAGE]
+                dense[pl.ds(column * SPAN + page * PAGE + leasts[k], PAGE), :] += tile
     for half in range(halves):
         lanes = pl.ds(half * 128, 128)
         weighted = jnp.zeros((turns, 128), jnp.float32)
@@ -417,21 +420,31 @@
         gathered, tops, ranks, live, hand_cards
     )
     blocks = swap(blocks, lines)
-    blocks = call(
-        run_sums, (PLANE, PAGE_ROWS, 128), [(LINE, BOARD_ROWS, 128), (PAGE_ROWS, 128)], blocks
-    )
-    blocks = swap(blocks, planes)
-    turn_out, flop_out, values, cards = pl.pallas_call(
-        lambda *refs: finish(*factors, *refs),
-        out_shape=outputs + (jax.ShapeDtypeStruct((1,), jnp.int32),),
-        in_specs=spread(3),
-        out_specs=tuple(spread(3)) + (pl.BlockSpec(memory_space=pltpu.SMEM),),
-        scratch_shapes=[pltpu.VMEM((actions * (width // 128) * SPAN, 128), f32)],
-        compiler_params=params,
-    )(blocks, by_action, flop_regret)
+    def page_of(past, boards_of_run):
+        shape, scratch = (PLANE, PAGE_ROWS, 128), [(LINE, BOARD_ROWS, 128), (PAGE_ROWS, 128)]
+        return swap(call(lambda *refs: run_sums(past, *refs), shape, scratch, boards_of_run), planes)
+
+    def results_of(*pages):
+        return pl.pallas_call(
+            lambda *refs: finish(*factors, len(pages), *refs),
+            out_shape=outputs + (jax.ShapeDtypeStruct((1,), jnp.int32),),
+            in_specs=spread(len(pages) + 2),
+            out_specs=tuple(spread(3)) + (pl.BlockSpec(memory_space=pltpu.SMEM),),
+            scratch_shapes=[pltpu.VMEM((actions * (width // 128) * SPAN, 128), f32)],
+            compiler_params=params,
+        )(*pages, by_action, flop_regret)
+
+    page = page_of(0.0, blocks)
+    turn_out, flop_out, values, cards = results_of(page)
+
+    def next_page(state):
+        again = blocks + jnp.where(state[0] > PAGE, 0, 1).astype(jnp.int16)
+        *results, held = results_of(page, page_of(float(PAGE), again))
+        state = lax.while_loop(lambda s: s[0] > 2 * PAGE, every_card, (held[0], *results))
+        return (jnp.int32(0),) + tuple(state[1:])
 
     def every_card(state):
-        payload = gathered + jnp.where(state[0] > PAGE, 0, 1).astype(jnp.int16)
+        payload = gathered + jnp.where(state[0] > 2 * PAGE, 0, 1).astype(jnp.int16)
         scratch = [(UNITS * 8, 128), gathered.shape]
         chunks = call(
             showdown_all, (PLANE, CHUNK, 128), scratch, payload, tops, ranks, live, hand_cards
@@ -450,7 +463,7 @@
         return (jnp.int32(0),) + tuple(results)
 
     state = (cards[0], turn_out, flop_out, values)
-    _, turn_out, flop_out, values = lax.while_loop(lambda s: s[0] > PAGE, every_card, state)
+    _, turn_out, flop_out, values = lax.while_loop(lambda s: s[0] > PAGE, next_page, state)
     return (jnp.transpose(turn_out, (1, 0, 2)), flop_out, values)
 
 

time: 65.6 us -> 65.6 us (level)
  no operation moved by 1% of the time
where the time goes in v10:
time: 65.6 us; the launch traced here: 65.3 us
  blocking collectives  59.2 us (90%)
  Pallas kernels  4.78 us (7%)
  between operations  0.71 us (1%)
    all_to_all x2, blocking collectives, swap(): lax.all_to_all(blocks, 'turn', 0, 0, axis_index_groups=groups, tiled=True)  42.5 us
    all_gather x1, blocking collectives, shards(): gathered = lax.all_gather(payload, 'hand', axis=0, tiled=False)  16.7 us
    pallas_call x2, Pallas kernels, call(): pl.pallas_call(kernel, out_shape=jax.ShapeDtypeStruct(shape, jnp.int16),...  1.97 us
    pallas_call x1, Pallas kernels, results_of(): pl.pallas_call(lambda *refs: finish(*factors, len(pages), *refs), out_sha...  1.56 us

profile of v10, /device:TPU:32, one launch (start us, length us, event | category | flops | bytes accessed | tf_op | source)
XLA Modules:
  0.0 65.3 jit_solution(2848009615927095927)
XLA Ops:
  0.6 1.3 %shard_map.121 = (s16[2,80,128]{2,1,0:T(8,128)(2,1)S(1)}, f32[24,128]{1,0:T(8,128)S(1)}) custom-call(f32[81]{0:T(128)} %pot_hbm.1, s32[81]{0:T(128)} %turn_hbm.1, s32[81]{0:T(128)} %flop_hbm.1, s32[4]{0:T(128)} %of_hbm.1, bf16[81,4,256]{2,1,0:T(4,128)(2,1)} %bitcast.13, s32[4,256]{1,0:T(4,128)} %ranks.1, s32[4,256]{1,0:T(4,128)} %live.1, f32[1,81]{1,0:T(1,128)} %bitcast.14, ...), custom_call_target="tpu_custom_call" | custom-call | tf_op jit(solution)/shard_map/pallas_call | solution.py:368
  1.9 0.0 copy-start.2
  1.9 0.0 copy-start.3
  1.9 0.0 copy-start.4
  1.9 16.7 %all-gather = s16[8,80,128]{2,1,0:T(8,128)(2,1)S(1)} all-gather(s16[2,80,128]{2,1,0:T(8,128)(2,1)S(1)} %get-tuple-element.138), channel_id=2, replica_groups=mesh['turn'=128,'hand'=4] {'hand'}, dimensions={0}, use_global_device_ids=true | all-gather | bytes 204800 | tf_op jit(solution)/shard_map/all_gather | solution.py:392
  18.6 0.0 copy-done.2
  18.6 0.0 copy-done.3
  18.6 0.0 copy-done.4
  18.6 1.3 %shard_map.122 = s16[8,96,128]{2,1,0:T(8,128)(2,1)S(1)} custom-call(s16[4,2,80,128]{3,2,1,0:T(8,128)(2,1)S(1)} %bitcast.11, f32[24,128]{1,0:T(8,128)S(1)} %get-tuple-element.261.tops, s32[4,256]{1,0:T(4,128)S(1)} %copy-done.3, s32[4,256]{1,0:T(4,128)S(1)} %copy-done.4, s32[2,1024]{1,0:T(2,128)S(1)} %copy-done.2), custom_call_target="tpu_custom_call" | custom-call | tf_op jit(solution)/shard_map/pallas_call | solution.py:406
  19.9 24.1 %all_to_all.30.refs_0_ = s16[8,96,128]{2,1,0:T(8,128)(2,1)S(1)} all-to-all(s16[8,96,128]{2,1,0:T(8,128)(2,1)S(1)} %shard_map.122), channel_id=1, replica_groups={{0,4,8,12,16,20,24,28},{32,36,40,44,48,52,56,60},{64,68,72,76,80,84,88,..., dimensions={0} | all-to-all | bytes 393216 | tf_op jit(solution)/shard_map/all_to_all | solution.py:416
  44.0 0.7 %shard_map.123 = s16[16,176,128]{2,1,0:T(8,128)(2,1)S(1)} custom-call(s16[8,96,128]{2,1,0:T(8,128)(2,1)S(1)} %all_to_all.30.refs_0_), custom_call_target="tpu_custom_call" | custom-call | tf_op jit(solution)/shard_map/pallas_call | solution.py:406
  44.7 0.0 copy-start
  44.7 0.0 copy-start.1
  44.7 18.4 %all_to_all.31.refs_0_ = s16[16,176,128]{2,1,0:T(8,128)(2,1)S(1)} all-to-all(s16[16,176,128]{2,1,0:T(8,128)(2,1)S(1)} %shard_map.123), channel_id=1, replica_groups={{0,32,64,96,128,160,192,224,256,288,320,352,384,416,448,480},{4,36,68,1..., dimensions={0} | all-to-all | bytes 1441792 | tf_op jit(solution)/shard_map/all_to_all | solution.py:416
  63.1 0.0 copy-done
  63.1 0.0 copy-done.1
  63.1 1.6 %shard_map.124 = (f32[9,49,256]{2,1,0:T(8,128)}, f32[9,256]{1,0:T(8,128)}, f32[49,256]{1,0:T(8,128)}, s32[1]{0:T(128)}) custom-call(s16[16,176,128]{2,1,0:T(8,128)(2,1)S(1)} %all_to_all.31.refs_0_, f32[9,49,256]{2,1,0:T(8,128)S(1)} %bitcast.9, f32[9,256]{1,0:T(8,128)S(1)} %copy-done.1), custom_call_target="tpu_custom_call" | custom-call | tf_op jit(solution)/shard_map/pallas_call | solution.py:428
  64.7 0.6 while.26
Async XLA Ops:
  1.9 16.7 %copy-start.2 = (s32[2,1024]{1,0:T(2,128)S(1)}, s32[2,1024]{1,0:T(2,128)}, u32[]{:S(2)}) copy-start(s32[2,1024]{1,0:T(2,128)} %cards.1) | copy-start | bytes 24580
  1.9 16.7 %copy-start.3 = (s32[4,256]{1,0:T(4,128)S(1)}, s32[4,256]{1,0:T(4,128)}, u32[]{:S(2)}) copy-start(s32[4,256]{1,0:T(4,128)} %ranks.1) | copy-start | bytes 12292
  1.9 16.7 %copy-start.4 = (s32[4,256]{1,0:T(4,128)S(1)}, s32[4,256]{1,0:T(4,128)}, u32[]{:S(2)}) copy-start(s32[4,256]{1,0:T(4,128)} %live.1) | copy-start | bytes 12292
  44.7 18.4 %copy-start = (f32[49,9,256]{2,0,1:T(8,128)S(1)}, f32[49,9,256]{2,0,1:T(8,128)}, u32[]{:S(2)}) copy-start(f32[49,9,256]{2,0,1:T(8,128)} %param.22) | copy-start | bytes 1354756
  44.7 18.4 %copy-start.1 = (f32[9,256]{1,0:T(8,128)S(1)}, f32[9,256]{1,0:T(8,128)}, u32[]{:S(2)}) copy-start(f32[9,256]{1,0:T(8,128)} %refs_2_.1) | copy-start | bytes 27652

commit v11 on v10

--- a/solution.py
+++ b/solution.py
@@ -463,7 +463,7 @@
         return (jnp.int32(0),) + tuple(results)
 
     state = (cards[0], turn_out, flop_out, values)
-    _, turn_out, flop_out, values = lax.while_loop(lambda s: s[0] > PAGE, next_page, state)
+    _, turn_out, flop_out, values = lax.cond(state[0] > PAGE, next_page, lambda s: s, state)
     return (jnp.transpose(turn_out, (1, 0, 2)), flop_out, values)
 
 

time: 65.6 us -> 65.6 us (level)
  no operation moved by 1% of the time
where the time goes in v11:
time: 65.6 us; the launch traced here: 65.3 us
  blocking collectives  59.2 us (90%)
  Pallas kernels  4.78 us (7%)
  between operations  1.34 us (2%)
    all_to_all x2, blocking collectives, swap(): lax.all_to_all(blocks, 'turn', 0, 0, axis_index_groups=groups, tiled=True)  42.5 us
    all_gather x1, blocking collectives, shards(): gathered = lax.all_gather(payload, 'hand', axis=0, tiled=False)  16.7 us
    pallas_call x2, Pallas kernels, call(): pl.pallas_call(kernel, out_shape=jax.ShapeDtypeStruct(shape, jnp.int16),...  1.97 us
    pallas_call x1, Pallas kernels, results_of(): pl.pallas_call(lambda *refs: finish(*factors, len(pages), *refs), out_sha...  1.56 us

profile of v11, /device:TPU:32, one launch (start us, length us, event | category | flops | bytes accessed | tf_op | source)
XLA Modules:
  0.0 65.3 jit_solution(13001546055685102456)
XLA Ops:
  0.6 1.3 %shard_map.121 = (s16[2,80,128]{2,1,0:T(8,128)(2,1)S(1)}, f32[24,128]{1,0:T(8,128)S(1)}) custom-call(f32[81]{0:T(128)} %pot_hbm.1, s32[81]{0:T(128)} %turn_hbm.1, s32[81]{0:T(128)} %flop_hbm.1, s32[4]{0:T(128)} %of_hbm.1, bf16[81,4,256]{2,1,0:T(4,128)(2,1)} %bitcast.13, s32[4,256]{1,0:T(4,128)} %ranks.1, s32[4,256]{1,0:T(4,128)} %live.1, f32[1,81]{1,0:T(1,128)} %bitcast.14, ...), custom_call_target="tpu_custom_call" | custom-call | tf_op jit(solution)/shard_map/pallas_call | solution.py:368
  1.9 0.0 copy-start.2
  1.9 0.0 copy-start.3
  1.9 0.0 copy-start.4
  1.9 16.7 %all-gather = s16[8,80,128]{2,1,0:T(8,128)(2,1)S(1)} all-gather(s16[2,80,128]{2,1,0:T(8,128)(2,1)S(1)} %get-tuple-element.111), channel_id=2, replica_groups=mesh['turn'=128,'hand'=4] {'hand'}, dimensions={0}, use_global_device_ids=true | all-gather | bytes 204800 | tf_op jit(solution)/shard_map/all_gather | solution.py:392
  18.6 0.0 copy-done.2
  18.6 0.0 copy-done.3
  18.6 0.0 copy-done.4
  18.6 1.3 %shard_map.122 = s16[8,96,128]{2,1,0:T(8,128)(2,1)S(1)} custom-call(s16[4,2,80,128]{3,2,1,0:T(8,128)(2,1)S(1)} %bitcast.11, f32[24,128]{1,0:T(8,128)S(1)} %get-tuple-element.112.tops, s32[4,256]{1,0:T(4,128)S(1)} %copy-done.3, s32[4,256]{1,0:T(4,128)S(1)} %copy-done.4, s32[2,1024]{1,0:T(2,128)S(1)} %copy-done.2), custom_call_target="tpu_custom_call" | custom-call | tf_op jit(solution)/shard_map/pallas_call | solution.py:406
  19.9 24.1 %all_to_all.30.refs_0_ = s16[8,96,128]{2,1,0:T(8,128)(2,1)S(1)} all-to-all(s16[8,96,128]{2,1,0:T(8,128)(2,1)S(1)} %shard_map.122), channel_id=1, replica_groups={{0,4,8,12,16,20,24,28},{32,36,40,44,48,52,56,60},{64,68,72,76,80,84,88,..., dimensions={0} | all-to-all | bytes 393216 | tf_op jit(solution)/shard_map/all_to_all | solution.py:416
  44.0 0.7 %shard_map.123 = s16[16,176,128]{2,1,0:T(8,128)(2,1)S(1)} custom-call(s16[8,96,128]{2,1,0:T(8,128)(2,1)S(1)} %all_to_all.30.refs_0_), custom_call_target="tpu_custom_call" | custom-call | tf_op jit(solution)/shard_map/pallas_call | solution.py:406
  44.7 0.0 copy-start
  44.7 0.0 copy-start.1
  44.7 18.4 %all_to_all.31.refs_0_ = s16[16,176,128]{2,1,0:T(8,128)(2,1)S(1)} all-to-all(s16[16,176,128]{2,1,0:T(8,128)(2,1)S(1)} %shard_map.123), channel_id=1, replica_groups={{0,32,64,96,128,160,192,224,256,288,320,352,384,416,448,480},{4,36,68,1..., dimensions={0} | all-to-all | bytes 1441792 | tf_op jit(solution)/shard_map/all_to_all | solution.py:416
  63.1 0.0 copy-done
  63.1 0.0 copy-done.1
  63.1 1.6 %shard_map.124 = (f32[9,49,256]{2,1,0:T(8,128)}, f32[9,256]{1,0:T(8,128)}, f32[49,256]{1,0:T(8,128)}, s32[1]{0:T(128)}) custom-call(s16[16,176,128]{2,1,0:T(8,128)(2,1)S(1)} %all_to_all.31.refs_0_, f32[9,49,256]{2,1,0:T(8,128)S(1)} %bitcast.9, f32[9,256]{1,0:T(8,128)S(1)} %copy-done.1), custom_call_target="tpu_custom_call" | custom-call | tf_op jit(solution)/shard_map/pallas_call | solution.py:428
  (1 shorter events, 0.0 us)
Async XLA Ops:
  1.9 16.7 %copy-start.2 = (s32[2,1024]{1,0:T(2,128)S(1)}, s32[2,1024]{1,0:T(2,128)}, u32[]{:S(2)}) copy-start(s32[2,1024]{1,0:T(2,128)} %cards.1) | copy-start | bytes 24580
  1.9 16.7 %copy-start.3 = (s32[4,256]{1,0:T(4,128)S(1)}, s32[4,256]{1,0:T(4,128)}, u32[]{:S(2)}) copy-start(s32[4,256]{1,0:T(4,128)} %ranks.1) | copy-start | bytes 12292
  1.9 16.7 %copy-start.4 = (s32[4,256]{1,0:T(4,128)S(1)}, s32[4,256]{1,0:T(4,128)}, u32[]{:S(2)}) copy-start(s32[4,256]{1,0:T(4,128)} %live.1) | copy-start | bytes 12292
  44.7 18.4 %copy-start = (f32[49,9,256]{2,0,1:T(8,128)S(1)}, f32[49,9,256]{2,0,1:T(8,128)}, u32[]{:S(2)}) copy-start(f32[49,9,256]{2,0,1:T(8,128)} %param.22) | copy-start | bytes 1354756
  44.7 18.4 %copy-start.1 = (f32[9,256]{1,0:T(8,128)S(1)}, f32[9,256]{1,0:T(8,128)}, u32[]{:S(2)}) copy-start(f32[9,256]{1,0:T(8,128)} %refs_2_.1) | copy-start | bytes 27652
